TPU v7x, 32 devices: a whole 2x2x4 slice. The times are simulated.
32 devices in a mesh: strip: 8 (over z, core), pt: 4 (over y, x).
Axes of the slice: x: 2, y: 2, z: 4, core: 2. Of those that a mesh axis runs over, the one named last changes fastest.
Arguments:
- spectra: float32 [600, 32, 1024], P(None, 'strip', 'pt'), may hold values from 0.01 to 1
- courant: float32 [25], replicated, may hold values from 0.05 to 0.4
- wind_speed: float32 [32, 1024], P('strip', 'pt'), may hold values from 0.5 to 2
- wind_dir: float32 [32, 1024], P('strip', 'pt'), may hold values from -3.140625 to 3.140625
- sea_mask: int32 [32, 1024], P('strip', 'pt'), may hold values 0 or 1
- ice_mask: int32 [32, 1024], P('strip', 'pt'), may hold values 0 or 1
Outputs:
- new_spectra: float32 [600, 32, 1024], P(None, 'strip', 'pt')
All inputs are finite; a program needn't handle non-finite values. No bound on the sum of `sea_mask` or of `ice_mask` on one device may be relied on, other than what follows from the above.
Results may differ from a plain program's by a relative error of at most 0.000088.
Values sent between devices are 32-bit elements; how exact they have to be, the bound alone decides.
A program may use at most 64 MiB of HBM per device.

v0:
```python
import jax
import jax.numpy as jnp
from jax import lax
from jax.sharding import PartitionSpec as P

NF = 25
ND = 24
SUB = 2


def with_halo(block, sides, width):
    for axis, dim in sides:
        count = lax.axis_size(axis)
        forward = [(i, i + 1) for i in range(count - 1)]
        backward = [(target, source) for source, target in forward]
        low = lax.ppermute(
            lax.slice_in_dim(block, block.shape[dim] - width, None, axis=dim), axis, forward
        )
        high = lax.ppermute(lax.slice_in_dim(block, 0, width, axis=dim), axis, backward)
        block = jnp.concatenate([low, block, high], axis=dim)
    return block


def tables(courant):
    ratio = 1.1 ** jnp.arange(NF, dtype=jnp.float32)
    theta = 2.0 * jnp.pi * jnp.arange(ND, dtype=jnp.float32) / ND
    speed_u = (courant[:, None] * jnp.cos(theta)[None, :]).reshape(-1)
    speed_v = (courant[:, None] * jnp.sin(theta)[None, :]).reshape(-1)
    return (ratio, theta, speed_u, speed_v)


def advance(core, west, east, south, north, speed_u, speed_v, sea):
    up_pos = jnp.maximum(speed_u, 0.0)[:, None, None]
    up_neg = jnp.minimum(speed_u, 0.0)[:, None, None]
    vp_pos = jnp.maximum(speed_v, 0.0)[:, None, None]
    vp_neg = jnp.minimum(speed_v, 0.0)[:, None, None]
    fresh = (
        core
        - up_pos * (core - west)
        - up_neg * (east - core)
        - vp_pos * (core - south)
        - vp_neg * (north - core)
    )
    return fresh * sea


def source(energy, wind_speed, wind_dir, ice_mask, ratio, theta):
    rows = energy.shape[1]
    cols = energy.shape[2]
    field = energy.reshape(NF, ND, rows, cols)
    weight = ratio / (ND * jnp.sum(ratio))
    first = jnp.einsum("fdyx,f->yx", field, weight, precision=lax.Precision.HIGHEST)
    second = jnp.einsum("fdyx,f->yx", field, weight * ratio, precision=lax.Precision.HIGHEST)
    mean_ratio = second / jnp.maximum(first, 0.05)
    icef = ice_mask.astype(jnp.float32)
    align = jnp.maximum(jnp.cos(theta[:, None, None] - wind_dir[None]), 0.0)
    gain = 0.05 * wind_speed[None, None] * ratio[:, None, None, None] * align[None]
    loss = 0.02 * ratio[:, None, None, None] * mean_ratio[None, None]
    net = (1.0 - icef)[None, None] * gain - loss - 0.7 * icef[None, None]
    return (field * jnp.exp(net)).reshape(NF * ND, rows, cols)


def advance_rows(field, speed_u, speed_v, sea_core):
    core = field[:, 1:-1]
    return advance(
        core,
        jnp.roll(core, 1, axis=2),
        jnp.roll(core, -1, axis=2),
        field[:, :-2],
        field[:, 2:],
        speed_u,
        speed_v,
        sea_core[None],
    )


def on_device(spectra, courant, wind_speed, wind_dir, sea_mask, ice_mask):
    ratio, theta, speed_u, speed_v = tables(courant)
    total = spectra.shape[0]
    rows = spectra.shape[1]
    groups = lax.axis_size("pt")
    per_dev = -(-total // groups)
    padded_total = per_dev * groups
    padded = spectra
    speed_u_all = speed_u
    speed_v_all = speed_v
    if padded_total > total:
        extra = padded_total - total
        padded = jnp.concatenate(
            [spectra, jnp.zeros((extra, rows, spectra.shape[2]), jnp.float32)], axis=0
        )
        speed_u_all = jnp.concatenate([speed_u, jnp.zeros((extra,), jnp.float32)])
        speed_v_all = jnp.concatenate([speed_v, jnp.zeros((extra,), jnp.float32)])
    fields = lax.all_to_all(padded, "pt", split_axis=0, concat_axis=2, tiled=True)
    start = lax.axis_index("pt") * per_dev
    local_u = lax.dynamic_slice_in_dim(speed_u_all, start, per_dev)
    local_v = lax.dynamic_slice_in_dim(speed_v_all, start, per_dev)
    sea_whole = lax.all_gather(sea_mask, "pt", axis=1, tiled=True).astype(jnp.float32)
    for step in range(SUB):
        wide = with_halo(fields, (("strip", 1),), 1)
        fields = advance_rows(wide, local_u, local_v, sea_whole)
    energy = lax.all_to_all(fields, "pt", split_axis=2, concat_axis=0, tiled=True)[:total]
    return source(energy, wind_speed, wind_dir, ice_mask, ratio, theta)


def solution(mesh):
    in_specs = (
        P(None, "strip", "pt"),
        P(),
        P("strip", "pt"),
        P("strip", "pt"),
        P("strip", "pt"),
        P("strip", "pt"),
    )
    out_specs = P(None, "strip", "pt")
    return jax.shard_map(
        on_device, mesh=mesh, in_specs=in_specs, out_specs=out_specs, check_vma=False
    )
```

profile of v0, /device:TPU:9, one launch (start us, length us, event | category | flops | bytes accessed | tf_op | source)
XLA Modules:
  0.0 145.8 jit_solution(4126674702477734589)
XLA Ops:
  0.0 3.8 %all-to-all-start = ((f32[600,4,256]{2,1,0:T(4,128)}), f32[600,4,256]{2,1,0:T(4,128)S(1)}, u32[]{:S(2)}, u32[]{:S(2)}) async-start(f32[600,4,256]{2,1,0:T(4,128)} %param.6), calls=%async_computation | async-start | bytes 4915200 | tf_op jit(solution)/shard_map/all_to_all | solution.py:94
  4.1 29.0 %all_gather.3 = s32[4,1024]{1,0:T(4,128)S(1)} all-gather(s32[4,256]{1,0:T(4,128)S(1)} %copy-done), channel_id=1, replica_groups=mesh['strip'=8,'pt'=4] {'pt'}, dimensions={1}, use_global_device_ids=true | all-gather | bytes 20480 | tf_op jit(solution)/shard_map/all_gather | solution.py:98
  33.3 2.4 %copy.34 = f32[4,150,4,256]{3,0,1,2:T(4,128)} copy(f32[4,150,4,256]{3,2,1,0:T(4,128)S(1)} %bitcast.41) | data formatting | bytes 4915200 | tf_op jit(solution)/shard_map/all_to_all | solution.py:94
  35.7 2.6 %all_to_all.27 = f32[150,4,1024]{2,0,1:T(8,128)S(1)} reshape(f32[150,4,4,256]{3,2,0,1:T(4,128)} %bitcast.42) | data formatting | bytes 4915200 | tf_op jit(solution)/shard_map/all_to_all | solution.py:94
  39.0 5.1 %collective-permute-start = (f32[150,1,1024]{2,1,0:T(1,128)S(1)}, f32[150,1,1024]{2,1,0:T(1,128)S(1)}, u32[]{:S(2)}, u32[]{:S(2)}) collective-permute-start(f32[150,1,1024]{2,1,0:T(1,128)S(1)} %copy.13), channel_id=1, source_target_pairs={{0,4},{4,8},{8,12},{12,16},{16,20},{20,24},{24,28},{1,5},{5,9},{9,... | collective-permute-start | bytes 1843208 | tf_op jit(solution)/shard_map/ppermute | solution.py:16
  44.7 1.9 %collective-permute-start.1 = (f32[150,1,1024]{2,1,0:T(1,128)S(1)}, f32[150,1,1024]{2,1,0:T(1,128)S(1)}, u32[]{:S(2)}, u32[]{:S(2)}) collective-permute-start(f32[150,1,1024]{2,1,0:T(1,128)S(1)} %copy.15), channel_id=1, source_target_pairs={{4,0},{8,4},{12,8},{16,12},{20,16},{24,20},{28,24},{5,1},{9,5},{13... | collective-permute-start | bytes 1843208 | tf_op jit(solution)/shard_map/ppermute | solution.py:19
  47.7 3.4 %collective-permute-done = f32[150,1,1024]{2,1,0:T(1,128)S(1)} collective-permute-done((f32[150,1,1024]{2,1,0:T(1,128)S(1)}, f32[150,1,1024]{2,1,0:T(1,128)S(1)}, u32[]{:S(2)}, u32[]{:S(2)}) %collective-permute-start) | collective-permute-done | bytes 614432 | tf_op jit(solution)/shard_map/ppermute | solution.py:16
  51.2 4.9 %collective-permute-done.1 = f32[150,1,1024]{2,1,0:T(1,128)S(1)} collective-permute-done((f32[150,1,1024]{2,1,0:T(1,128)S(1)}, f32[150,1,1024]{2,1,0:T(1,128)S(1)}, u32[]{:S(2)}, u32[]{:S(2)}) %collective-permute-start.1) | collective-permute-done | bytes 614432 | tf_op jit(solution)/shard_map/ppermute | solution.py:19
  56.3 2.4 %fusion.10 = f32[150,4,1024]{2,0,1:T(8,128)S(1)} fusion(f32[150,4,1024]{2,0,1:T(8,128)S(1)} %all_to_all.27, f32[150,1,1024]{2,0,1:T(8,128)S(1)} %copy.16, f32[150,1,1024]{2,0,1:T(8,128)S(1)} %copy.14, f32[150,4,1023]{2,0,1:T(8,128)S(1)} %get-tuple-element.12, f32[150,4,1]{2,0,1:T(8,128)S(1)} %get-tuple-element.14, f32[150,4,1]{2,0,1:T(8,128)S(1)} %get-tuple-element.13, ...), kind=kLoop, calls=%fused_computation.13 | loop fusion | flops 10444800 | bytes 11077984 | tf_op jit(solution)/shard_map/mul | solution.py:44
  59.4 1.9 %collective-permute-start.2 = (f32[150,1,1024]{2,1,0:T(1,128)S(1)}, f32[150,1,1024]{2,1,0:T(1,128)S(1)}, u32[]{:S(2)}, u32[]{:S(2)}) collective-permute-start(f32[150,1,1024]{2,1,0:T(1,128)S(1)} %copy.17), channel_id=1, source_target_pairs={{0,4},{4,8},{8,12},{12,16},{16,20},{20,24},{24,28},{1,5},{5,9},{9,... | collective-permute-start | bytes 1843208 | tf_op jit(solution)/shard_map/ppermute | solution.py:16
  62.0 2.4 %collective-permute-start.3 = (f32[150,1,1024]{2,1,0:T(1,128)S(1)}, f32[150,1,1024]{2,1,0:T(1,128)S(1)}, u32[]{:S(2)}, u32[]{:S(2)}) collective-permute-start(f32[150,1,1024]{2,1,0:T(1,128)S(1)} %copy.19), channel_id=1, source_target_pairs={{4,0},{8,4},{12,8},{16,12},{20,16},{24,20},{28,24},{5,1},{9,5},{13... | collective-permute-start | bytes 1843208 | tf_op jit(solution)/shard_map/ppermute | solution.py:19
  65.5 2.8 %collective-permute-done.2 = f32[150,1,1024]{2,1,0:T(1,128)S(1)} collective-permute-done((f32[150,1,1024]{2,1,0:T(1,128)S(1)}, f32[150,1,1024]{2,1,0:T(1,128)S(1)}, u32[]{:S(2)}, u32[]{:S(2)}) %collective-permute-start.2) | collective-permute-done | bytes 614432 | tf_op jit(solution)/shard_map/ppermute | solution.py:16
  68.5 4.9 %collective-permute-done.3 = f32[150,1,1024]{2,1,0:T(1,128)S(1)} collective-permute-done((f32[150,1,1024]{2,1,0:T(1,128)S(1)}, f32[150,1,1024]{2,1,0:T(1,128)S(1)}, u32[]{:S(2)}, u32[]{:S(2)}) %collective-permute-start.3) | collective-permute-done | bytes 614432 | tf_op jit(solution)/shard_map/ppermute | solution.py:19
  73.5 2.4 %fusion.3 = f32[150,4,1024]{2,0,1:T(8,128)S(1)} fusion(f32[150,4,1024]{2,0,1:T(8,128)S(1)} %fusion.10, f32[150,1,1024]{2,0,1:T(8,128)S(1)} %copy.20, f32[150,1,1024]{2,0,1:T(8,128)S(1)} %copy.18, f32[150,4,1023]{2,0,1:T(8,128)S(1)} %get-tuple-element.6, f32[150,4,1]{2,0,1:T(8,128)S(1)} %get-tuple-element.8, f32[150,4,1]{2,0,1:T(8,128)S(1)} %get-tuple-element.7, ...), kind=kLoop, calls=%fused_computation.4 | loop fusion | flops 10444800 | bytes 11077984 | tf_op jit(solution)/shard_map/mul | solution.py:44
  75.9 3.2 %copy.21 = f32[150,4,1024]{0,1,2:T(4,128)} copy(f32[150,4,1024]{2,0,1:T(8,128)S(1)} %fusion.3) | data formatting | bytes 4915200 | tf_op jit(solution)/shard_map/mul | solution.py:44
  79.1 5.2 %all-to-all-start.1 = ((f32[150,4,1024]{0,1,2:T(4,128)}), f32[150,4,1024]{0,1,2:T(4,128)}, u32[]{:S(2)}, u32[]{:S(2)}) async-start(f32[150,4,1024]{0,1,2:T(4,128)} %copy.21), calls=%async_computation.1 | async-start | bytes 8388608 | tf_op jit(solution)/shard_map/all_to_all | solution.py:102
  86.1 1.7 %broadcast_multiply_fusion = f32[25,24,4,256]{3,1,0,2:T(8,128)} fusion(f32[24,4,256]{2,0,1:T(8,128)S(1)} %cosine_maximum_fusion, f32[25,4,256]{2,0,1:T(8,128)S(1)} %broadcast_multiply_fusion.2), kind=kLoop, calls=%fused_computation.36 | loop fusion | flops 614400 | bytes 2658304 | tf_op jit(solution)/shard_map/mul | solution.py:57
  87.9 43.4 %all-to-all-done.1 = f32[150,4,1024]{0,1,2:T(4,128)} async-done(((f32[150,4,1024]{0,1,2:T(4,128)}), f32[150,4,1024]{0,1,2:T(4,128)}, u32[]{:S(2)}, u32[]{:S(2)}) %all-to-all-start.1) | async-done | bytes 2457632 | tf_op jit(solution)/shard_map/all_to_all | solution.py:102
  131.2 3.5 %copy.23 = f32[4,150,4,256]{3,1,0,2:T(8,128)S(1)} copy(f32[4,150,4,256]{1,2,3,0:T(4,128)} %bitcast.4) | data formatting | bytes 4915200 | tf_op jit(solution)/shard_map/all_to_all | solution.py:102
  134.7 1.6 %reshape.69 = f32[25,24,4,256]{3,1,0,2:T(8,128)} reshape(f32[4,150,4,256]{3,1,0,2:T(8,128)S(1)} %copy.23) | data formatting | bytes 4915200 | tf_op jit(solution)/shard_map/reshape | solution.py:50
  136.3 2.0 %reduce_sum.16 = f32[25,4,256]{2,0,1:T(8,128)S(1)} reduce(f32[25,24,4,256]{3,1,0,2:T(8,128)} %reshape.69, f32[]{:T(128)} %constant.3.clone.1), dimensions={1}, to_apply=%region_0.1 | reduce | flops 588800 | bytes 2560004 | tf_op jit(solution)/shard_map/fdyx,f->yx/reduce_sum | solution.py:53
  138.8 1.6 %reshape.68 = f32[600,4,256]{2,0,1:T(8,128)} reshape(f32[4,150,4,256]{3,1,0,2:T(8,128)S(1)} %copy.23) | data formatting | bytes 4915200 | tf_op jit(solution)/shard_map/reshape | solution.py:50
  140.4 2.9 %fusion.24 = f32[600,4,256]{2,0,1:T(8,128)S(1)} fusion(f32[600,4,256]{2,0,1:T(8,128)} %reshape.68, f32[25,24,4,256]{3,1,0,2:T(8,128)} %broadcast_multiply_fusion, f32[4,256]{1,0:T(4,128)S(1)} %get-tuple-element.18, f32[25,4,256]{2,0,1:T(8,128)S(1)} %broadcast_multiply_fusion.1, f32[4,256]{1,0:T(4,128)S(1)} %get-tuple-element.17), kind=kLoop, calls=%fused_computation.33 | loop fusion | flops 2457600 | bytes 7483392 | tf_op jit(solution)/shard_map/mul | solution.py:60
  143.4 2.4 %copy.25 = f32[600,4,256]{2,1,0:T(4,128)} copy(f32[600,4,256]{2,0,1:T(8,128)S(1)} %fusion.24) | data formatting | bytes 4915200 | tf_op jit(solution)/shard_map/mul | solution.py:60
  (44 shorter events, 7.4 us)
Async XLA Ops:
  0.0 3.8 %copy-start.4 = (f32[25]{0:T(128)S(1)}, f32[25]{0:T(128)}, u32[]{:S(2)}) copy-start(f32[25]{0:T(128)} %param.7) | copy-start | bytes 304
  0.0 4.1 %copy-start = (s32[4,256]{1,0:T(4,128)S(1)}, s32[4,256]{1,0:T(4,128)}, u32[]{:S(2)}) copy-start(s32[4,256]{1,0:T(4,128)} %param.10) | copy-start | bytes 12292
  0.0 33.3 %all-to-all-start = ((f32[600,4,256]{2,1,0:T(4,128)}), f32[600,4,256]{2,1,0:T(4,128)S(1)}, u32[]{:S(2)}, u32[]{:S(2)}) async-start(f32[600,4,256]{2,1,0:T(4,128)} %param.6), calls=%async_computation | async-start | bytes 4915200 | tf_op jit(solution)/shard_map/all_to_all | solution.py:94
  39.0 12.1 %collective-permute-start = (f32[150,1,1024]{2,1,0:T(1,128)S(1)}, f32[150,1,1024]{2,1,0:T(1,128)S(1)}, u32[]{:S(2)}, u32[]{:S(2)}) collective-permute-start(f32[150,1,1024]{2,1,0:T(1,128)S(1)} %copy.13), channel_id=1, source_target_pairs={{0,4},{4,8},{8,12},{12,16},{16,20},{20,24},{24,28},{1,5},{5,9},{9,... | collective-permute-start | bytes 1843208 | tf_op jit(solution)/shard_map/ppermute | solution.py:16
  44.7 11.5 %collective-permute-start.1 = (f32[150,1,1024]{2,1,0:T(1,128)S(1)}, f32[150,1,1024]{2,1,0:T(1,128)S(1)}, u32[]{:S(2)}, u32[]{:S(2)}) collective-permute-start(f32[150,1,1024]{2,1,0:T(1,128)S(1)} %copy.15), channel_id=1, source_target_pairs={{4,0},{8,4},{12,8},{16,12},{20,16},{24,20},{28,24},{5,1},{9,5},{13... | collective-permute-start | bytes 1843208 | tf_op jit(solution)/shard_map/ppermute | solution.py:19
  59.4 9.0 %collective-permute-start.2 = (f32[150,1,1024]{2,1,0:T(1,128)S(1)}, f32[150,1,1024]{2,1,0:T(1,128)S(1)}, u32[]{:S(2)}, u32[]{:S(2)}) collective-permute-start(f32[150,1,1024]{2,1,0:T(1,128)S(1)} %copy.17), channel_id=1, source_target_pairs={{0,4},{4,8},{8,12},{12,16},{16,20},{20,24},{24,28},{1,5},{5,9},{9,... | collective-permute-start | bytes 1843208 | tf_op jit(solution)/shard_map/ppermute | solution.py:16
  62.0 11.5 %collective-permute-start.3 = (f32[150,1,1024]{2,1,0:T(1,128)S(1)}, f32[150,1,1024]{2,1,0:T(1,128)S(1)}, u32[]{:S(2)}, u32[]{:S(2)}) collective-permute-start(f32[150,1,1024]{2,1,0:T(1,128)S(1)} %copy.19), channel_id=1, source_target_pairs={{4,0},{8,4},{12,8},{16,12},{20,16},{24,20},{28,24},{5,1},{9,5},{13... | collective-permute-start | bytes 1843208 | tf_op jit(solution)/shard_map/ppermute | solution.py:19
  79.1 6.5 %copy-start.3 = (f32[4,256]{1,0:T(4,128)S(1)}, f32[4,256]{1,0:T(4,128)}, u32[]{:S(2)}) copy-start(f32[4,256]{1,0:T(4,128)} %param.8) | copy-start | bytes 12292
  79.1 6.5 %copy-start.1 = (s32[4,256]{1,0:T(4,128)S(1)}, s32[4,256]{1,0:T(4,128)}, u32[]{:S(2)}) copy-start(s32[4,256]{1,0:T(4,128)} %param.11) | copy-start | bytes 12292
  79.1 6.5 %copy-start.2 = (f32[4,256]{1,0:T(4,128)S(1)}, f32[4,256]{1,0:T(4,128)}, u32[]{:S(2)}) copy-start(f32[4,256]{1,0:T(4,128)} %param.9) | copy-start | bytes 12292
  79.1 52.1 %all-to-all-start.1 = ((f32[150,4,1024]{0,1,2:T(4,128)}), f32[150,4,1024]{0,1,2:T(4,128)}, u32[]{:S(2)}, u32[]{:S(2)}) async-start(f32[150,4,1024]{0,1,2:T(4,128)} %copy.21), calls=%async_computation.1 | async-start | bytes 8388608 | tf_op jit(solution)/shard_map/all_to_all | solution.py:102
where the time goes:
time: 146 us
  waiting for transfers between devices  59.5 us (41%)
  blocking collectives  29 us (20%)
  local copies, waits for them, and re-layouts  22.8 us (16%)
  starting transfers between devices  20.2 us (14%)
  other arithmetic  12.9 us (9%)
    all_to_all x1, waiting for transfers between devices, on_device(): lax.all_to_all(fields, 'pt', split_axis=2, concat_axis=0, tiled=True)  43.4 us
    all_gather x1, blocking collectives, on_device(): lax.all_gather(sea_mask, 'pt', axis=1, tiled=True).astype(jnp.float32)  29 us
    ppermute x2, waiting for transfers between devices, with_halo(): lax.ppermute(lax.slice_in_dim(block, 0, width, axis=dim), axis, backward)  9.84 us
    ppermute x2, starting transfers between devices, with_halo(): lax.ppermute(lax.slice_in_dim(block, block.shape[dim] - width, None, axis...  6.97 us
    ppermute x2, waiting for transfers between devices, with_halo(): lax.ppermute(lax.slice_in_dim(block, block.shape[dim] - width, None, axis...  6.27 us
    all_to_all x1, starting transfers between devices, on_device(): lax.all_to_all(fields, 'pt', split_axis=2, concat_axis=0, tiled=True)  5.16 us
    all_to_all x2, local copies, waits for them, and re-layouts, on_device(): lax.all_to_all(padded, 'pt', split_axis=0, concat_axis=2, tiled=True)  4.97 us
    mul x2, other arithmetic, advance(): return fresh * sea  4.72 us
  transfers between devices with their start and end apart: 6, of which 5 were waited for; matrix products, arithmetic and copies ran while one was open for 5% of the time, Pallas kernels for 0%

commit v1 on v0

v1 whole, which is shorter than its diff:
```python
import functools
import numpy as np
import jax
import jax.numpy as jnp
from jax import lax
from jax.experimental import pallas as pl
from jax.experimental.pallas import tpu as pltpu
from jax.sharding import PartitionSpec as P

NF = 25
ND = 24
HALF = ND // 2
CH = 5
IC = NF // CH
RPI = ND * 8
RPC = RPI * IC
MESH = pl.DeviceIdType.MESH

THETA = (np.float32(2.0 * np.pi) * np.arange(ND, dtype=np.float32) / np.float32(ND)).astype(np.float32)
COS = np.cos(THETA).astype(np.float32)
SIN = np.sin(THETA).astype(np.float32)
RATIO = np.float32(1.1) ** np.arange(NF, dtype=np.float32)
WEIGHT = (RATIO / (ND * np.sum(RATIO, dtype=np.float64))).astype(np.float32)
FROM_WEST = [d for d in range(ND) if COS[d] > 0.0]
FROM_EAST = [d for d in range(ND) if not COS[d] > 0.0]


def pieces():
    return ((0, 0, 8, 0), (0, 8, 4, 8), (1, 0, 4, 12), (1, 4, 8, 16))


def kernel(
    n_strip, n_pt,
    table, courant, wind_speed, wind_dir, sea_mask, ice_mask, spectra,
    out,
    e0, e1, gain, row_send, row_recv, col_send, col_recv,
    in_sem, out_sem, send_sem, recv_sem,
):
    s = lax.axis_index("strip")
    p = lax.axis_index("pt")
    east = lax.rem(p + 1, n_pt)
    west = lax.rem(p + n_pt - 1, n_pt)
    has_south = s > 0
    has_north = s < n_strip - 1

    def load(c):
        rows = pl.ds(pl.multiple_of(c * RPC, RPC), RPC)
        return pltpu.make_async_copy(spectra.at[rows, :], e0.at[rows, :], in_sem.at[c])

    def store(c):
        rows = pl.ds(pl.multiple_of(c * RPC, RPC), RPC)
        return pltpu.make_async_copy(e1.at[rows, :], out.at[rows, :], out_sem.at[c])

    def rows_to(phase, c, way):
        return pltpu.make_async_remote_copy(
            src_ref=row_send.at[phase, c, way],
            dst_ref=row_recv.at[phase, c, way],
            send_sem=send_sem.at[phase, c, way],
            recv_sem=recv_sem.at[phase, c, way],
            device_id={"strip": s + 1 if way == 0 else s - 1},
            device_id_type=MESH,
        )

    def cols_to(phase, c, way):
        return pltpu.make_async_remote_copy(
            src_ref=col_send.at[phase, c],
            dst_ref=col_recv.at[phase, c, way],
            send_sem=send_sem.at[phase, c, 2 + way],
            recv_sem=recv_sem.at[phase, c, 2 + way],
            device_id={"pt": east if way == 0 else west},
            device_id_type=MESH,
        )

    def send(phase, c):
        @pl.when(has_north)
        def _():
            rows_to(phase, c, 0).start()

        @pl.when(has_south)
        def _():
            rows_to(phase, c, 1).start()

        cols_to(phase, c, 0).start()
        cols_to(phase, c, 1).start()

    def receive(phase, c):
        cols_to(phase, c, 0).wait_recv()
        cols_to(phase, c, 1).wait_recv()

        @pl.when(has_south)
        def _():
            rows_to(phase, c, 0).wait_recv()

        @pl.when(has_north)
        def _():
            rows_to(phase, c, 1).wait_recv()

    for c in range(CH):
        load(c).start()

    barrier = pltpu.get_barrier_semaphore()
    for side in (east, west):
        pl.semaphore_signal(barrier, inc=1, device_id={"pt": side}, device_id_type=MESH)

    @pl.when(has_north)
    def _():
        pl.semaphore_signal(barrier, inc=1, device_id={"strip": s + 1}, device_id_type=MESH)

    @pl.when(has_south)
    def _():
        pl.semaphore_signal(barrier, inc=1, device_id={"strip": s - 1}, device_id_type=MESH)

    @pl.when(jnp.logical_not(has_south))
    def _():
        row_recv[:, :, 0] = jnp.zeros(row_recv.shape[:2] + row_recv.shape[3:], jnp.float32)

    @pl.when(jnp.logical_not(has_north))
    def _():
        row_recv[:, :, 1] = jnp.zeros(row_recv.shape[:2] + row_recv.shape[3:], jnp.float32)

    lane = lax.broadcasted_iota(jnp.int32, (8, 128), 1)
    sub = lax.broadcasted_iota(jnp.int32, (8, 128), 0)
    low = sub < 4
    first_lane = lane == 0
    last_lane = lane == 127
    sea = sea_mask[...].astype(jnp.float32)
    ice = ice_mask[...].astype(jnp.float32)

    def pack_rows(src, phase, c):
        def one(il, carry):
            base = pl.multiple_of((c * IC + il) * RPI, 8)
            to = pl.multiple_of(il * ND, 8)
            for tile, first, count, at in pieces():
                up = src[pl.ds(base + first * 8 + 3 + 4 * tile, count, stride=8), :]
                row_send[phase, c, 0, pl.ds(to + at, count), :] = up
                down = src[pl.ds(base + (HALF + first) * 8 + 4 * tile, count, stride=8), :]
                row_send[phase, c, 1, pl.ds(to + at, count), :] = down
            return carry

        lax.fori_loop(0, IC, one, 0)

    def put(acc, m, rolled_pos, neg):
        mixed = jnp.where(low, neg, rolled_pos)
        if m:
            mixed = pltpu.roll(mixed, m, 1)
        return jnp.where(lane == m, mixed, acc)

    pl.semaphore_wait(
        barrier, 2 + has_north.astype(jnp.int32) + has_south.astype(jnp.int32)
    )

    def first_halo(c, carry):
        load(c).wait()
        pack_rows(e0, 0, c)

        def one(il, acc):
            base = pl.multiple_of((c * IC + il) * RPI, 8)
            own = jnp.zeros((8, 128), jnp.float32)
            for m in range(HALF):
                pos = e0[pl.ds(base + 8 * FROM_WEST[m], 8), :]
                neg = e0[pl.ds(base + 8 * FROM_EAST[m], 8), :]
                own = put(own, m, pltpu.roll(pos, 1, 1), neg)
            return jnp.where(lane < HALF, own, pltpu.roll(acc, HALF, 1))

        col_send[0, c] = lax.fori_loop(0, IC, one, jnp.zeros((8, 128), jnp.float32))
        send(0, c)
        return carry

    lax.fori_loop(0, CH, first_halo, 0)

    strength = (1.0 - ice) * 0.05 * wind_speed[...]
    cos_wind = jnp.cos(wind_dir[...])
    sin_wind = jnp.sin(wind_dir[...])
    for d in range(ND):
        align = jnp.maximum(float(COS[d]) * cos_wind + float(SIN[d]) * sin_wind, 0.0)
        gain[pl.ds(8 * d, 8), :] = strength * align

    def advance(src, dst, phase, c, sums):
        receive(phase, c)
        halo = pltpu.roll(jnp.where(low, col_recv[phase, c, 1], col_recv[phase, c, 0]), 4, 0)
        halo = pltpu.roll(halo, 128 - (IC - 1) * HALF, 1)

        def one(il, carry):
            halo, acc, m0, m1 = carry
            i = c * IC + il
            base = pl.multiple_of(i * RPI, 8)
            at = pl.multiple_of(il * ND, 8)
            speed = courant[i] * sea
            keep = [sea - speed * float(k) for k in (np.abs(COS[:4]) + np.abs(SIN[:4]))]
            own = jnp.zeros((8, 128), jnp.float32)
            total = jnp.zeros((8, 128), jnp.float32)

            def step(d, core, side):
                if d < HALF:
                    near = pltpu.roll(core, 1, 0)
                    r0, r1, way, m = 0, 4, 0, d
                else:
                    near = pltpu.roll(core, 7, 0)
                    r0, r1, way, m = 3, 7, 1, d - HALF
                h0 = row_recv[phase, c, way, pl.ds(at + m, 1), :]
                h1 = row_recv[phase, c, way, pl.ds(at + HALF + m, 1), :]
                near = jnp.where(sub == r0, h0, jnp.where(sub == r1, h1, near))
                flow = float(abs(COS[d])) * side + float(abs(SIN[d])) * near
                q = d % 6
                fresh = keep[q if q < 4 else 6 - q] * core + speed * flow
                dst[pl.ds(base + 8 * d, 8), :] = fresh
                return fresh

            for m in range(HALF):
                pos = src[pl.ds(base + 8 * FROM_WEST[m], 8), :]
                neg = src[pl.ds(base + 8 * FROM_EAST[m], 8), :]
                edge = jnp.broadcast_to(halo[:, m : m + 1], (8, 128))
                rolled_pos = pltpu.roll(pos, 1, 1)
                rolled_neg = pltpu.roll(neg, 127, 1)
                swap = pltpu.roll(jnp.where(first_lane, rolled_pos, rolled_neg), 4, 0)
                side_pos = jnp.where(first_lane, jnp.where(low, edge, swap), rolled_pos)
                side_neg = jnp.where(last_lane, jnp.where(low, swap, edge), rolled_neg)
                new_pos = step(FROM_WEST[m], pos, side_pos)
                new_neg = step(FROM_EAST[m], neg, side_neg)
                if phase == 0:
                    own = put(own, m, pltpu.roll(new_pos, 1, 1), new_neg)
                else:
                    total = total + (new_pos + new_neg)
            if phase == 0:
                acc = jnp.where(lane < HALF, own, pltpu.roll(acc, HALF, 1))
            else:
                m0 = m0 + table[1, i] * total
                m1 = m1 + table[2, i] * total
            return pltpu.roll(halo, HALF, 1), acc, m0, m1

        zero = jnp.zeros((8, 128), jnp.float32)
        _, acc, m0, m1 = lax.fori_loop(0, IC, one, (halo, zero) + sums)
        if phase == 0:
            col_send[1, c] = acc
            pack_rows(dst, 1, c)
            send(1, c)
        return m0, m1

    zero = jnp.zeros((8, 128), jnp.float32)

    def first_step(c, carry):
        advance(e0, e1, 0, c, (zero, zero))
        return carry

    lax.fori_loop(0, CH, first_step, 0)
    m0, m1 = lax.fori_loop(
        0, CH, lambda c, sums: advance(e1, e0, 1, c, sums), (zero, zero)
    )
    mean_ratio = m1 / jnp.maximum(m0, 0.05)
    drag = 0.02 * mean_ratio
    cold = 0.7 * ice

    def last(c, carry):
        def one(il, carry):
            i = c * IC + il
            base = pl.multiple_of(i * RPI, 8)
            ratio = table[0, i]
            loss = ratio * drag + cold
            for d in range(ND):
                rows = pl.ds(base + 8 * d, 8)
                e1[rows, :] = e0[rows, :] * jnp.exp(ratio * gain[pl.ds(8 * d, 8), :] - loss)
            return carry

        lax.fori_loop(0, IC, one, 0)
        store(c).start()
        return carry

    lax.fori_loop(0, CH, last, 0)

    def finish(c, carry):
        for phase in range(2):
            @pl.when(has_north)
            def _():
                rows_to(phase, c, 0).wait_send()

            @pl.when(has_south)
            def _():
                rows_to(phase, c, 1).wait_send()

            cols_to(phase, c, 0).wait_send()
            cols_to(phase, c, 1).wait_send()
        store(c).wait()
        return carry

    lax.fori_loop(0, CH, finish, 0)


def to_tiles(x):
    lead, rows, cols = x.shape
    x = x.reshape(lead, rows, cols // 128, 128).transpose(0, 2, 1, 3)
    return x.reshape(lead * rows * cols // 128, 128)


def from_tiles(x, shape):
    lead, rows, cols = shape
    x = x.reshape(lead, cols // 128, rows, 128).transpose(0, 2, 1, 3)
    return x.reshape(shape)


def on_device(n_strip, n_pt, spectra, courant, wind_speed, wind_dir, sea_mask, ice_mask):
    table = jnp.asarray(np.stack([RATIO, WEIGHT, WEIGHT * RATIO]))
    total = spectra.shape[0] * 8
    vmem = pl.BlockSpec(memory_space=pltpu.VMEM)
    smem = pl.BlockSpec(memory_space=pltpu.SMEM)
    hbm = pl.BlockSpec(memory_space=pl.ANY)
    sem = pltpu.SemaphoreType.DMA
    rows = IC * ND
    result = pl.pallas_call(
        functools.partial(kernel, n_strip, n_pt),
        out_shape=jax.ShapeDtypeStruct((total, 128), jnp.float32),
        in_specs=[smem, smem, vmem, vmem, vmem, vmem, hbm],
        out_specs=hbm,
        scratch_shapes=[
            pltpu.VMEM((total, 128), jnp.float32),
            pltpu.VMEM((total, 128), jnp.float32),
            pltpu.VMEM((ND * 8, 128), jnp.float32),
            pltpu.VMEM((2, CH, 2, rows, 128), jnp.float32),
            pltpu.VMEM((2, CH, 2, rows, 128), jnp.float32),
            pltpu.VMEM((2, CH, 8, 128), jnp.float32),
            pltpu.VMEM((2, CH, 2, 8, 128), jnp.float32),
            sem((CH,)),
            sem((CH,)),
            sem((2, CH, 4)),
            sem((2, CH, 4)),
        ],
        compiler_params=pltpu.CompilerParams(
            collective_id=0, has_side_effects=True, vmem_limit_bytes=32 * 1024 * 1024
        ),
        cost_estimate=pl.CostEstimate(
            flops=40 * total * 128, bytes_accessed=8 * total * 128, transcendentals=total * 128
        ),
    )(
        table,
        courant,
        to_tiles(wind_speed[None]),
        to_tiles(wind_dir[None]),
        to_tiles(sea_mask[None]),
        to_tiles(ice_mask[None]),
        to_tiles(spectra),
    )
    return from_tiles(result, spectra.shape)


def solution(mesh):
    in_specs = (
        P(None, "strip", "pt"),
        P(),
        P("strip", "pt"),
        P("strip", "pt"),
        P("strip", "pt"),
        P("strip", "pt"),
    )
    return jax.shard_map(
        functools.partial(on_device, mesh.shape["strip"], mesh.shape["pt"]),
        mesh=mesh,
        in_specs=in_specs,
        out_specs=P(None, "strip", "pt"),
        check_vma=False,
    )
```

time: 146 us -> 32 us (0.22)
  the two profiles are of different devices: /device:TPU:9 before, /device:TPU:1 now
where the time goes in v1:
time: 32 us; the launch traced here: 31.7 us
  Pallas kernels  24.4 us (76%)
  local copies, waits for them, and re-layouts  7.21 us (23%)
    pallas_call x1, Pallas kernels, on_device(): pl.pallas_call(functools.partial(kernel, n_strip, n_pt), out_shape=jax.Sh...  24.4 us
    unnamed x15, local copies, waits for them, and re-layouts  7.21 us

profile of v1, /device:TPU:1, one launch (start us, length us, event | category | flops | bytes accessed | tf_op | source)
XLA Modules:
  0.0 31.7 jit_solution(8262474111020650997)
XLA Ops:
  0.0 0.0 copy-start
  0.0 1.7 %copy-done = f32[600,4,256]{2,1,0:T(4,128)S(1)} copy-done((f32[600,4,256]{2,1,0:T(4,128)S(1)}, f32[600,4,256]{2,1,0:T(4,128)}, u32[]{:S(2)}) %copy-start) | copy-done | bytes 2457624
  1.7 0.0 copy-start.1
  1.7 0.7 %copy-done.1 = f32[4,256]{1,0:T(4,128)S(1)} copy-done((f32[4,256]{1,0:T(4,128)S(1)}, f32[4,256]{1,0:T(4,128)}, u32[]{:S(2)}) %copy-start.1) | copy-done | bytes 4120
  2.4 0.0 copy-start.2
  2.4 0.7 %copy-done.2 = f32[4,256]{1,0:T(4,128)S(1)} copy-done((f32[4,256]{1,0:T(4,128)S(1)}, f32[4,256]{1,0:T(4,128)}, u32[]{:S(2)}) %copy-start.2) | copy-done | bytes 4120
  3.1 0.0 copy-start.3
  3.1 0.7 %copy-done.3 = s32[4,256]{1,0:T(4,128)S(1)} copy-done((s32[4,256]{1,0:T(4,128)S(1)}, s32[4,256]{1,0:T(4,128)}, u32[]{:S(2)}) %copy-start.3) | copy-done | bytes 4120
  3.8 0.0 copy-start.4
  3.8 0.7 %copy-done.4 = s32[4,256]{1,0:T(4,128)S(1)} copy-done((s32[4,256]{1,0:T(4,128)S(1)}, s32[4,256]{1,0:T(4,128)}, u32[]{:S(2)}) %copy-start.4) | copy-done | bytes 4120
  4.4 0.0 copy-start.5
  4.4 0.7 %copy-done.5 = f32[3,25]{1,0:T(4,128)S(1)} copy-done((f32[3,25]{1,0:T(4,128)S(1)}, f32[3,25]{1,0:T(4,128)}, u32[]{:S(2)}) %copy-start.5) | copy-done | bytes 324
  5.1 0.0 copy-start.6
  5.1 0.7 %copy-done.6 = f32[25]{0:T(128)S(1)} copy-done((f32[25]{0:T(128)S(1)}, f32[25]{0:T(128)}, u32[]{:S(2)}) %copy-start.6) | copy-done | bytes 124
  5.8 24.4 %shard_map.73 = f32[4800,128]{1,0:T(8,128)S(1)} custom-call(f32[3,25]{1,0:T(4,128)S(1)} %copy-done.5, f32[25]{0:T(128)S(1)} %copy-done.6, f32[8,128]{1,0:T(8,128)S(1)} %bitcast.32, f32[8,128]{1,0:T(8,128)S(1)} %bitcast.33, s32[8,128]{1,0:T(8,128)S(1)} %bitcast.34, s32[8,128]{1,0:T(8,128)S(1)} %bitcast.35, f32[4800,128]{1,0:T(8,128)S(1)} %bitcast.31), custom_call_target="tpu_custom_call" | custom-call | flops 24576000 | bytes 4915200 | tf_op jit(solution)/shard_map/pallas_call | solution.py:308
  30.2 1.4 %copy.15 = f32[600,4,256]{2,1,0:T(4,128)} copy(f32[600,4,256]{2,1,0:T(4,128)S(1)} %bitcast.30) | data formatting | bytes 4915200
Async XLA Ops:
  0.0 1.7 %copy-start = (f32[600,4,256]{2,1,0:T(4,128)S(1)}, f32[600,4,256]{2,1,0:T(4,128)}, u32[]{:S(2)}) copy-start(f32[600,4,256]{2,1,0:T(4,128)} %param.7) | copy-start | bytes 7372804
  1.7 0.7 %copy-start.1 = (f32[4,256]{1,0:T(4,128)S(1)}, f32[4,256]{1,0:T(4,128)}, u32[]{:S(2)}) copy-start(f32[4,256]{1,0:T(4,128)} %param.9) | copy-start | bytes 12292
  2.4 0.7 %copy-start.2 = (f32[4,256]{1,0:T(4,128)S(1)}, f32[4,256]{1,0:T(4,128)}, u32[]{:S(2)}) copy-start(f32[4,256]{1,0:T(4,128)} %param.10) | copy-start | bytes 12292
  3.1 0.7 %copy-start.3 = (s32[4,256]{1,0:T(4,128)S(1)}, s32[4,256]{1,0:T(4,128)}, u32[]{:S(2)}) copy-start(s32[4,256]{1,0:T(4,128)} %param.11) | copy-start | bytes 12292
  3.8 0.7 %copy-start.4 = (s32[4,256]{1,0:T(4,128)S(1)}, s32[4,256]{1,0:T(4,128)}, u32[]{:S(2)}) copy-start(s32[4,256]{1,0:T(4,128)} %param.12) | copy-start | bytes 12292
  4.4 0.7 %copy-start.5 = (f32[3,25]{1,0:T(4,128)S(1)}, f32[3,25]{1,0:T(4,128)}, u32[]{:S(2)}) copy-start(f32[3,25]{1,0:T(4,128)} %constant.2.clone.table) | copy-start | bytes 904
  5.1 0.7 %copy-start.6 = (f32[25]{0:T(128)S(1)}, f32[25]{0:T(128)}, u32[]{:S(2)}) copy-start(f32[25]{0:T(128)} %courant.1) | copy-start | bytes 304

commit v2 on v1

--- a/solution.py
+++ b/solution.py
@@ -31,10 +31,11 @@
 
 def kernel(
     n_strip, n_pt,
-    table, courant, wind_speed, wind_dir, sea_mask, ice_mask, spectra,
-    out,
-    e0, e1, gain, row_send, row_recv, col_send, col_recv,
-    in_sem, out_sem, send_sem, recv_sem,
+    courant_in, sea_in, spectra,
+    out, mean_ratio,
+    e0, e1, sea_mask, courant, table,
+    row_send, row_recv, col_send, col_recv,
+    in_sem, out_sem, small_sem, send_sem, recv_sem,
 ):
     s = lax.axis_index("strip")
     p = lax.axis_index("pt")
@@ -49,7 +50,7 @@
 
     def store(c):
         rows = pl.ds(pl.multiple_of(c * RPC, RPC), RPC)
-        return pltpu.make_async_copy(e1.at[rows, :], out.at[rows, :], out_sem.at[c])
+        return pltpu.make_async_copy(e0.at[rows, :], out.at[rows, :], out_sem.at[c])
 
     def rows_to(phase, c, way):
         return pltpu.make_async_remote_copy(
@@ -95,8 +96,19 @@
         def _():
             rows_to(phase, c, 1).wait_recv()
 
+    smalls = [
+        pltpu.make_async_copy(source, target, small_sem.at[n])
+        for n, (source, target) in enumerate(
+            ((courant_in, courant), (sea_in, sea_mask))
+        )
+    ]
     for c in range(CH):
         load(c).start()
+    for small in smalls:
+        small.start()
+    for i in range(NF):
+        table[0, i] = float(WEIGHT[i])
+        table[1, i] = float(WEIGHT[i] * RATIO[i])
 
     barrier = pltpu.get_barrier_semaphore()
     for side in (east, west):
@@ -123,8 +135,6 @@
     low = sub < 4
     first_lane = lane == 0
     last_lane = lane == 127
-    sea = sea_mask[...].astype(jnp.float32)
-    ice = ice_mask[...].astype(jnp.float32)
 
     def pack_rows(src, phase, c):
         def one(il, carry):
@@ -137,7 +147,7 @@
                 row_send[phase, c, 1, pl.ds(to + at, count), :] = down
             return carry
 
-        lax.fori_loop(0, IC, one, 0)
+        lax.fori_loop(0, IC, one, 0, unroll=True)
 
     def put(acc, m, rolled_pos, neg):
         mixed = jnp.where(low, neg, rolled_pos)
@@ -162,18 +172,17 @@
                 own = put(own, m, pltpu.roll(pos, 1, 1), neg)
             return jnp.where(lane < HALF, own, pltpu.roll(acc, HALF, 1))
 
-        col_send[0, c] = lax.fori_loop(0, IC, one, jnp.zeros((8, 128), jnp.float32))
+        col_send[0, c] = lax.fori_loop(
+            0, IC, one, jnp.zeros((8, 128), jnp.float32), unroll=True
+        )
         send(0, c)
         return carry
 
     lax.fori_loop(0, CH, first_halo, 0)
 
-    strength = (1.0 - ice) * 0.05 * wind_speed[...]
-    cos_wind = jnp.cos(wind_dir[...])
-    sin_wind = jnp.sin(wind_dir[...])
-    for d in range(ND):
-        align = jnp.maximum(float(COS[d]) * cos_wind + float(SIN[d]) * sin_wind, 0.0)
-        gain[pl.ds(8 * d, 8), :] = strength * align
+    for small in smalls:
+        small.wait()
+    sea = sea_mask[...].astype(jnp.float32)
 
     def advance(src, dst, phase, c, sums):
         receive(phase, c)
@@ -224,12 +233,12 @@
             if phase == 0:
                 acc = jnp.where(lane < HALF, own, pltpu.roll(acc, HALF, 1))
             else:
-                m0 = m0 + table[1, i] * total
-                m1 = m1 + table[2, i] * total
+                m0 = m0 + table[0, i] * total
+                m1 = m1 + table[1, i] * total
             return pltpu.roll(halo, HALF, 1), acc, m0, m1
 
         zero = jnp.zeros((8, 128), jnp.float32)
-        _, acc, m0, m1 = lax.fori_loop(0, IC, one, (halo, zero) + sums)
+        _, acc, m0, m1 = lax.fori_loop(0, IC, one, (halo, zero) + sums, unroll=True)
         if phase == 0:
             col_send[1, c] = acc
             pack_rows(dst, 1, c)
@@ -243,29 +252,13 @@
         return carry
 
     lax.fori_loop(0, CH, first_step, 0)
-    m0, m1 = lax.fori_loop(
-        0, CH, lambda c, sums: advance(e1, e0, 1, c, sums), (zero, zero)
-    )
-    mean_ratio = m1 / jnp.maximum(m0, 0.05)
-    drag = 0.02 * mean_ratio
-    cold = 0.7 * ice
-
-    def last(c, carry):
-        def one(il, carry):
-            i = c * IC + il
-            base = pl.multiple_of(i * RPI, 8)
-            ratio = table[0, i]
-            loss = ratio * drag + cold
-            for d in range(ND):
-                rows = pl.ds(base + 8 * d, 8)
-                e1[rows, :] = e0[rows, :] * jnp.exp(ratio * gain[pl.ds(8 * d, 8), :] - loss)
-            return carry
-
-        lax.fori_loop(0, IC, one, 0)
+    def second_step(c, sums):
+        sums = advance(e1, e0, 1, c, sums)
         store(c).start()
-        return carry
-
-    lax.fori_loop(0, CH, last, 0)
+        return sums
+
+    m0, m1 = lax.fori_loop(0, CH, second_step, (zero, zero))
+    mean_ratio[...] = m1 / jnp.maximum(m0, 0.05)
 
     def finish(c, carry):
         for phase in range(2):
@@ -285,6 +278,67 @@
     lax.fori_loop(0, CH, finish, 0)
 
 
+def source_kernel(
+    wind_speed_in, wind_dir_in, ice_in, mean_ratio_in, energy,
+    out,
+    held, done, wind_speed, wind_dir, ice_mask, mean_ratio, gain,
+    in_sem, out_sem, small_sem,
+):
+    loads = [
+        pltpu.make_async_copy(
+            energy.at[pl.ds(c * RPC, RPC), :], held.at[pl.ds(c * RPC, RPC), :], in_sem.at[c]
+        )
+        for c in range(CH)
+    ]
+    stores = [
+        pltpu.make_async_copy(
+            done.at[pl.ds(c * RPC, RPC), :], out.at[pl.ds(c * RPC, RPC), :], out_sem.at[c]
+        )
+        for c in range(CH)
+    ]
+    smalls = [
+        pltpu.make_async_copy(source, target, small_sem.at[n])
+        for n, (source, target) in enumerate(
+            (
+                (wind_dir_in, wind_dir),
+                (wind_speed_in, wind_speed),
+                (ice_in, ice_mask),
+                (mean_ratio_in, mean_ratio),
+            )
+        )
+    ]
+    for copy in smalls + loads:
+        copy.start()
+    for copy in smalls:
+        copy.wait()
+    ice = ice_mask[...].astype(jnp.float32)
+    strength = (1.0 - ice) * 0.05 * wind_speed[...]
+    cos_wind = strength * jnp.cos(wind_dir[...])
+    sin_wind = strength * jnp.sin(wind_dir[...])
+    for d in range(ND):
+        gain[pl.ds(8 * d, 8), :] = jnp.maximum(
+            float(COS[d]) * cos_wind + float(SIN[d]) * sin_wind, 0.0
+        )
+    drag = 0.02 * mean_ratio[...]
+    cold = 0.7 * ice
+    for c in range(CH):
+        loads[c].wait()
+        losses = [float(RATIO[c * IC + il]) * drag + cold for il in range(IC)]
+
+        def one(d, carry):
+            push = gain[pl.ds(pl.multiple_of(8 * d, 8), 8), :]
+            for il in range(IC):
+                rows = pl.ds(pl.multiple_of((c * IC + il) * RPI + 8 * d, 8), 8)
+                net = float(RATIO[c * IC + il]) * push - losses[il]
+                done[rows, :] = held[rows, :] * jnp.exp(net)
+            return carry
+
+        lax.fori_loop(0, ND, one, 0, unroll=8)
+        stores[c].start()
+    for copy in stores:
+        copy.wait()
+
+
 def to_tiles(x):
     lead, rows, cols = x.shape
     x = x.reshape(lead, rows, cols // 128, 128).transpose(0, 2, 1, 3)
@@ -298,45 +352,68 @@
 
 
 def on_device(n_strip, n_pt, spectra, courant, wind_speed, wind_dir, sea_mask, ice_mask):
-    table = jnp.asarray(np.stack([RATIO, WEIGHT, WEIGHT * RATIO]))
     total = spectra.shape[0] * 8
     vmem = pl.BlockSpec(memory_space=pltpu.VMEM)
-    smem = pl.BlockSpec(memory_space=pltpu.SMEM)
     hbm = pl.BlockSpec(memory_space=pl.ANY)
     sem = pltpu.SemaphoreType.DMA
     rows = IC * ND
-    result = pl.pallas_call(
+    whole = jax.ShapeDtypeStruct((total, 128), jnp.float32)
+    point = jax.ShapeDtypeStruct((8, 128), jnp.float32)
+    energy, mean_ratio = pl.pallas_call(
         functools.partial(kernel, n_strip, n_pt),
-        out_shape=jax.ShapeDtypeStruct((total, 128), jnp.float32),
-        in_specs=[smem, smem, vmem, vmem, vmem, vmem, hbm],
-        out_specs=hbm,
+        out_shape=[whole, point],
+        in_specs=[hbm] * 3,
+        out_specs=[hbm, vmem],
         scratch_shapes=[
             pltpu.VMEM((total, 128), jnp.float32),
             pltpu.VMEM((total, 128), jnp.float32),
-            pltpu.VMEM((ND * 8, 128), jnp.float32),
+            pltpu.VMEM((8, 128), jnp.int32),
+            pltpu.SMEM((NF,), jnp.float32),
+            pltpu.SMEM((2, NF), jnp.float32),
             pltpu.VMEM((2, CH, 2, rows, 128), jnp.float32),
             pltpu.VMEM((2, CH, 2, rows, 128), jnp.float32),
             pltpu.VMEM((2, CH, 8, 128), jnp.float32),
             pltpu.VMEM((2, CH, 2, 8, 128), jnp.float32),
             sem((CH,)),
             sem((CH,)),
+            sem((2,)),
             sem((2, CH, 4)),
             sem((2, CH, 4)),
         ],
         compiler_params=pltpu.CompilerParams(
-            collective_id=0, has_side_effects=True, vmem_limit_bytes=32 * 1024 * 1024
+            collective_id=0, has_side_effects=True, vmem_limit_bytes=60 * 1024 * 1024
         ),
         cost_estimate=pl.CostEstimate(
-            flops=40 * total * 128, bytes_accessed=8 * total * 128, transcendentals=total * 128
+            flops=30 * total * 128, bytes_accessed=8 * total * 128, transcendentals=0
+        ),
+    )(courant, to_tiles(sea_mask[None]), to_tiles(spectra))
+    result = pl.pallas_call(
+        source_kernel,
+        out_shape=whole,
+        in_specs=[hbm] * 5,
+        out_specs=hbm,
+        scratch_shapes=[
+            pltpu.VMEM((total, 128), jnp.float32),
+            pltpu.VMEM((total, 128), jnp.float32),
+            pltpu.VMEM((8, 128), jnp.float32),
+            pltpu.VMEM((8, 128), jnp.float32),
+            pltpu.VMEM((8, 128), jnp.int32),
+            pltpu.VMEM((8, 128), jnp.float32),
+            pltpu.VMEM((ND * 8, 128), jnp.float32),
+            sem((CH,)),
+            sem((CH,)),
+            sem((4,)),
+        ],
+        compiler_params=pltpu.CompilerParams(vmem_limit_bytes=60 * 1024 * 1024),
+        cost_estimate=pl.CostEstimate(
+            flops=4 * total * 128, bytes_accessed=8 * total * 128, transcendentals=total * 128
         ),
     )(
-        table,
-        courant,
         to_tiles(wind_speed[None]),
         to_tiles(wind_dir[None]),
-        to_tiles(sea_mask[None]),
         to_tiles(ice_mask[None]),
-        to_tiles(spectra),
+        mean_ratio,
+        energy,
     )
     return from_tiles(result, spectra.shape)
 

time: 32 us -> 19.7 us (0.62)
  local copies, waits for them, and re-layouts: 7.21 us -> 0 us
  Pallas kernels: 24.4 us -> 19.4 us
    unnamed x15 -> x0, local copies, waits for them, and re-layouts: 7.21 us -> none
    pallas_call x1 -> x2, Pallas kernels: 24.4 us -> 19.4 us  [the longest x1 16.3 us: on_device(): pl.pallas_call(functools.partial(kernel, n_strip, n_pt), out_shape=[whole...]
where the time goes in v2:
time: 19.7 us; the launch traced here: 19.4 us
  Pallas kernels  19.4 us (98%)
    pallas_call x1, Pallas kernels, on_device(): pl.pallas_call(functools.partial(kernel, n_strip, n_pt), out_shape=[whole...  16.3 us
    pallas_call x1, Pallas kernels, on_device(): pl.pallas_call(source_kernel, out_shape=whole, in_specs=[hbm] * 5, out_sp...  3.02 us

profile of v2, /device:TPU:1, one launch (start us, length us, event | category | flops | bytes accessed | tf_op | source)
XLA Modules:
  0.0 19.4 jit_solution(9975425490980171793)
XLA Ops:
  0.0 16.3 %shard_map.64 = (f32[4800,128]{1,0:T(8,128)}, f32[8,128]{1,0:T(8,128)}) custom-call(f32[25]{0:T(128)} %courant_in.1, s32[8,128]{1,0:T(8,128)} %bitcast.31, f32[4800,128]{1,0:T(8,128)} %bitcast.30), custom_call_target="tpu_custom_call" | custom-call | flops 18432000 | bytes 4915200 | tf_op jit(solution)/shard_map/pallas_call | solution.py:362
  16.4 3.0 %shard_map.65 = f32[4800,128]{1,0:T(8,128)} custom-call(f32[8,128]{1,0:T(8,128)} %bitcast.32, f32[8,128]{1,0:T(8,128)} %bitcast.33, s32[8,128]{1,0:T(8,128)} %bitcast.34, f32[8,128]{1,0:T(8,128)} %get-tuple-element.7.mean_ratio_in, f32[4800,128]{1,0:T(8,128)} %get-tuple-element.8.energy), custom_call_target="tpu_custom_call" | custom-call | flops 2457600 | bytes 4915200 | tf_op jit(solution)/shard_map/pallas_call | solution.py:390

commit v3 on v2

--- a/solution.py
+++ b/solution.py
@@ -33,7 +33,7 @@
     n_strip, n_pt,
     courant_in, sea_in, spectra,
     out, mean_ratio,
-    e0, e1, sea_mask, courant, table,
+    e0, e1, sea_mask, sea, courant, table, rise,
     row_send, row_recv, col_send, col_recv,
     in_sem, out_sem, small_sem, send_sem, recv_sem,
 ):
@@ -72,7 +72,7 @@
             device_id_type=MESH,
         )
 
-    def send(phase, c):
+    def send_rows(phase, c):
         @pl.when(has_north)
         def _():
             rows_to(phase, c, 0).start()
@@ -81,13 +81,11 @@
         def _():
             rows_to(phase, c, 1).start()
 
+    def send_cols(phase, c):
         cols_to(phase, c, 0).start()
         cols_to(phase, c, 1).start()
 
-    def receive(phase, c):
-        cols_to(phase, c, 0).wait_recv()
-        cols_to(phase, c, 1).wait_recv()
-
+    def receive_rows(phase, c):
         @pl.when(has_south)
         def _():
             rows_to(phase, c, 0).wait_recv()
@@ -95,6 +93,10 @@
         @pl.when(has_north)
         def _():
             rows_to(phase, c, 1).wait_recv()
+
+    def receive_cols(phase, c):
+        cols_to(phase, c, 0).wait_recv()
+        cols_to(phase, c, 1).wait_recv()
 
     smalls = [
         pltpu.make_async_copy(source, target, small_sem.at[n])
@@ -106,30 +108,33 @@
         load(c).start()
     for small in smalls:
         small.start()
+
+    barrier = pltpu.get_barrier_semaphore()
+    for side in (east, west):
+        pl.semaphore_signal(barrier, inc=1, device_id={"pt": side}, device_id_type=MESH)
+
+    @pl.when(has_north)
+    def _():
+        pl.semaphore_signal(barrier, inc=1, device_id={"strip": s + 1}, device_id_type=MESH)
+
+    @pl.when(has_south)
+    def _():
+        pl.semaphore_signal(barrier, inc=1, device_id={"strip": s - 1}, device_id_type=MESH)
+
+    @pl.when(jnp.logical_not(has_south))
+    def _():
+        row_recv[:, :, 0] = jnp.zeros(row_recv.shape[:2] + row_recv.shape[3:], jnp.float32)
+
+    @pl.when(jnp.logical_not(has_north))
+    def _():
+        row_recv[:, :, 1] = jnp.zeros(row_recv.shape[:2] + row_recv.shape[3:], jnp.float32)
+
     for i in range(NF):
         table[0, i] = float(WEIGHT[i])
         table[1, i] = float(WEIGHT[i] * RATIO[i])
-
-    barrier = pltpu.get_barrier_semaphore()
-    for side in (east, west):
-        pl.semaphore_signal(barrier, inc=1, device_id={"pt": side}, device_id_type=MESH)
-
-    @pl.when(has_north)
-    def _():
-        pl.semaphore_signal(barrier, inc=1, device_id={"strip": s + 1}, device_id_type=MESH)
-
-    @pl.when(has_south)
-    def _():
-        pl.semaphore_signal(barrier, inc=1, device_id={"strip": s - 1}, device_id_type=MESH)
-
-    @pl.when(jnp.logical_not(has_south))
-    def _():
-        row_recv[:, :, 0] = jnp.zeros(row_recv.shape[:2] + row_recv.shape[3:], jnp.float32)
-
-    @pl.when(jnp.logical_not(has_north))
-    def _():
-        row_recv[:, :, 1] = jnp.zeros(row_recv.shape[:2] + row_recv.shape[3:], jnp.float32)
-
+    for d in range(HALF):
+        rise[pl.ds(d, 1), :] = jnp.full((1, 128), float(abs(SIN[d])), jnp.float32)
+        rise[pl.ds(16 + d, 1), :] = jnp.full((1, 128), float(abs(SIN[HALF + d])), jnp.float32)
     lane = lax.broadcasted_iota(jnp.int32, (8, 128), 1)
     sub = lax.broadcasted_iota(jnp.int32, (8, 128), 0)
     low = sub < 4
@@ -155,48 +160,57 @@
             mixed = pltpu.roll(mixed, m, 1)
         return jnp.where(lane == m, mixed, acc)
 
-    pl.semaphore_wait(
-        barrier, 2 + has_north.astype(jnp.int32) + has_south.astype(jnp.int32)
-    )
-
-    def first_halo(c, carry):
-        load(c).wait()
-        pack_rows(e0, 0, c)
-
+    def pack_cols(src, phase, c):
         def one(il, acc):
             base = pl.multiple_of((c * IC + il) * RPI, 8)
             own = jnp.zeros((8, 128), jnp.float32)
             for m in range(HALF):
-                pos = e0[pl.ds(base + 8 * FROM_WEST[m], 8), :]
-                neg = e0[pl.ds(base + 8 * FROM_EAST[m], 8), :]
+                pos = src[pl.ds(base + 8 * FROM_WEST[m], 8), :]
+                neg = src[pl.ds(base + 8 * FROM_EAST[m], 8), :]
                 own = put(own, m, pltpu.roll(pos, 1, 1), neg)
             return jnp.where(lane < HALF, own, pltpu.roll(acc, HALF, 1))
 
-        col_send[0, c] = lax.fori_loop(
+        col_send[phase, c] = lax.fori_loop(
             0, IC, one, jnp.zeros((8, 128), jnp.float32), unroll=True
         )
-        send(0, c)
+
+    load(0).wait()
+    pack_cols(e0, 0, 0)
+    pack_rows(e0, 0, 0)
+    pl.semaphore_wait(
+        barrier, 2 + has_north.astype(jnp.int32) + has_south.astype(jnp.int32)
+    )
+    send_cols(0, 0)
+    send_rows(0, 0)
+
+    def first_halo(c, carry):
+        load(c).wait()
+        pack_cols(e0, 0, c)
+        send_cols(0, c)
+        pack_rows(e0, 0, c)
+        send_rows(0, c)
         return carry
 
-    lax.fori_loop(0, CH, first_halo, 0)
-
+    lax.fori_loop(1, CH, first_halo, 0)
     for small in smalls:
         small.wait()
-    sea = sea_mask[...].astype(jnp.float32)
+    sea[...] = sea_mask[...].astype(jnp.float32)
 
     def advance(src, dst, phase, c, sums):
-        receive(phase, c)
+        receive_cols(phase, c)
+        if phase == 1:
+            receive_rows(phase, c)
         halo = pltpu.roll(jnp.where(low, col_recv[phase, c, 1], col_recv[phase, c, 0]), 4, 0)
         halo = pltpu.roll(halo, 128 - (IC - 1) * HALF, 1)
+        sea_now = sea[...]
 
         def one(il, carry):
-            halo, acc, m0, m1 = carry
+            halo, m0, m1 = carry
             i = c * IC + il
             base = pl.multiple_of(i * RPI, 8)
             at = pl.multiple_of(il * ND, 8)
-            speed = courant[i] * sea
-            keep = [sea - speed * float(k) for k in (np.abs(COS[:4]) + np.abs(SIN[:4]))]
-            own = jnp.zeros((8, 128), jnp.float32)
+            speed = courant[i] * sea_now
+            keep = [sea_now - speed * float(k) for k in (np.abs(COS[:4]) + np.abs(SIN[:4]))]
             total = jnp.zeros((8, 128), jnp.float32)
 
             def step(d, core, side):
@@ -206,9 +220,12 @@
                 else:
                     near = pltpu.roll(core, 7, 0)
                     r0, r1, way, m = 3, 7, 1, d - HALF
-                h0 = row_recv[phase, c, way, pl.ds(at + m, 1), :]
-                h1 = row_recv[phase, c, way, pl.ds(at + HALF + m, 1), :]
-                near = jnp.where(sub == r0, h0, jnp.where(sub == r1, h1, near))
+                if phase == 0:
+                    near = jnp.where((sub == r0) | (sub == r1), 0.0, near)
+                else:
+                    h0 = row_recv[phase, c, way, pl.ds(at + m, 1), :]
+                    h1 = row_recv[phase, c, way, pl.ds(at + HALF + m, 1), :]
+                    near = jnp.where(sub == r0, h0, jnp.where(sub == r1, h1, near))
                 flow = float(abs(COS[d])) * side + float(abs(SIN[d])) * near
                 q = d % 6
                 fresh = keep[q if q < 4 else 6 - q] * core + speed * flow
@@ -226,32 +243,50 @@
                 side_neg = jnp.where(last_lane, jnp.where(low, swap, edge), rolled_neg)
                 new_pos = step(FROM_WEST[m], pos, side_pos)
                 new_neg = step(FROM_EAST[m], neg, side_neg)
-                if phase == 0:
-                    own = put(own, m, pltpu.roll(new_pos, 1, 1), new_neg)
-                else:
+                if phase == 1:
                     total = total + (new_pos + new_neg)
-            if phase == 0:
-                acc = jnp.where(lane < HALF, own, pltpu.roll(acc, HALF, 1))
-            else:
+            if phase == 1:
                 m0 = m0 + table[0, i] * total
                 m1 = m1 + table[1, i] * total
-            return pltpu.roll(halo, HALF, 1), acc, m0, m1
-
-        zero = jnp.zeros((8, 128), jnp.float32)
-        _, acc, m0, m1 = lax.fori_loop(0, IC, one, (halo, zero) + sums, unroll=True)
-        if phase == 0:
-            col_send[1, c] = acc
-            pack_rows(dst, 1, c)
-            send(1, c)
+            return pltpu.roll(halo, HALF, 1), m0, m1
+
+        _, m0, m1 = lax.fori_loop(0, IC, one, (halo,) + sums, unroll=True)
         return m0, m1
 
     zero = jnp.zeros((8, 128), jnp.float32)
 
     def first_step(c, carry):
         advance(e0, e1, 0, c, (zero, zero))
+        pack_rows(e1, 1, c)
+        send_rows(1, c)
         return carry
 
     lax.fori_loop(0, CH, first_step, 0)
+
+    def first_edge(c, carry):
+        receive_rows(0, c)
+
+        def one(il, carry):
+            i = c * IC + il
+            base = pl.multiple_of(i * RPI, 8)
+            at = pl.multiple_of(il * ND, 8)
+            for way in range(2):
+                for tile, first, count, to in pieces():
+                    row = 4 * tile + 3 * way
+                    rows = pl.ds(base + (HALF * way + first) * 8 + row, count, stride=8)
+                    speed = courant[i] * sea[pl.ds(row, 1), :]
+                    term = row_recv[0, c, way, pl.ds(at + to, count), :]
+                    term = term * rise[pl.ds(16 * way + first, count), :]
+                    e1[rows, :] = e1[rows, :] + speed * term
+            return carry
+
+        lax.fori_loop(0, IC, one, 0, unroll=True)
+        pack_cols(e1, 1, c)
+        send_cols(1, c)
+        return carry
+
+    lax.fori_loop(0, CH, first_edge, 0)
+
     def second_step(c, sums):
         sums = advance(e1, e0, 1, c, sums)
         store(c).start()
@@ -368,8 +403,10 @@
             pltpu.VMEM((total, 128), jnp.float32),
             pltpu.VMEM((total, 128), jnp.float32),
             pltpu.VMEM((8, 128), jnp.int32),
+            pltpu.VMEM((8, 128), jnp.float32),
             pltpu.SMEM((NF,), jnp.float32),
             pltpu.SMEM((2, NF), jnp.float32),
+            pltpu.VMEM((32, 128), jnp.float32),
             pltpu.VMEM((2, CH, 2, rows, 128), jnp.float32),
             pltpu.VMEM((2, CH, 2, rows, 128), jnp.float32),
             pltpu.VMEM((2, CH, 8, 128), jnp.float32),

time: 19.7 us -> 21.2 us (1.076)
  the two profiles are of different devices: /device:TPU:1 before, /device:TPU:0 now
where the time goes in v3:
time: 21.2 us; the launch traced here: 21 us
  Pallas kernels  21 us (99%)
    pallas_call x1, Pallas kernels, on_device(): pl.pallas_call(functools.partial(kernel, n_strip, n_pt), out_shape=[whole...  18 us
    pallas_call x1, Pallas kernels, on_device(): pl.pallas_call(source_kernel, out_shape=whole, in_specs=[hbm] * 5, out_sp...  3.02 us

profile of v3, /device:TPU:0, one launch (start us, length us, event | category | flops | bytes accessed | tf_op | source)
XLA Modules:
  0.0 21.0 jit_solution(15364457426278075480)
XLA Ops:
  0.0 18.0 %shard_map.64 = (f32[4800,128]{1,0:T(8,128)}, f32[8,128]{1,0:T(8,128)}) custom-call(f32[25]{0:T(128)} %courant_in.1, s32[8,128]{1,0:T(8,128)} %bitcast.31, f32[4800,128]{1,0:T(8,128)} %bitcast.30), custom_call_target="tpu_custom_call" | custom-call | flops 18432000 | bytes 4915200 | tf_op jit(solution)/shard_map/pallas_call | solution.py:397
  18.0 3.0 %shard_map.65 = f32[4800,128]{1,0:T(8,128)} custom-call(f32[8,128]{1,0:T(8,128)} %bitcast.32, f32[8,128]{1,0:T(8,128)} %bitcast.33, s32[8,128]{1,0:T(8,128)} %bitcast.34, f32[8,128]{1,0:T(8,128)} %get-tuple-element.7.mean_ratio_in, f32[4800,128]{1,0:T(8,128)} %get-tuple-element.8.energy), custom_call_target="tpu_custom_call" | custom-call | flops 2457600 | bytes 4915200 | tf_op jit(solution)/shard_map/pallas_call | solution.py:427

commit v4 on v2

--- a/solution.py
+++ b/solution.py
@@ -14,6 +14,7 @@
 IC = NF // CH
 RPI = ND * 8
 RPC = RPI * IC
+PAD = 8
 MESH = pl.DeviceIdType.MESH
 
 THETA = (np.float32(2.0 * np.pi) * np.arange(ND, dtype=np.float32) / np.float32(ND)).astype(np.float32)
@@ -23,10 +24,6 @@
 WEIGHT = (RATIO / (ND * np.sum(RATIO, dtype=np.float64))).astype(np.float32)
 FROM_WEST = [d for d in range(ND) if COS[d] > 0.0]
 FROM_EAST = [d for d in range(ND) if not COS[d] > 0.0]
-
-
-def pieces():
-    return ((0, 0, 8, 0), (0, 8, 4, 8), (1, 0, 4, 12), (1, 4, 8, 16))
 
 
 def kernel(
@@ -46,16 +43,18 @@
 
     def load(c):
         rows = pl.ds(pl.multiple_of(c * RPC, RPC), RPC)
-        return pltpu.make_async_copy(spectra.at[rows, :], e0.at[rows, :], in_sem.at[c])
+        held = pl.ds(pl.multiple_of(c * RPC + PAD, 8), RPC)
+        return pltpu.make_async_copy(spectra.at[rows, :], e0.at[held, :], in_sem.at[c])
 
     def store(c):
         rows = pl.ds(pl.multiple_of(c * RPC, RPC), RPC)
-        return pltpu.make_async_copy(e0.at[rows, :], out.at[rows, :], out_sem.at[c])
+        held = pl.ds(pl.multiple_of(c * RPC + PAD, 8), RPC)
+        return pltpu.make_async_copy(e0.at[held, :], out.at[rows, :], out_sem.at[c])
 
     def rows_to(phase, c, way):
         return pltpu.make_async_remote_copy(
             src_ref=row_send.at[phase, c, way],
-            dst_ref=row_recv.at[phase, c, way],
+            dst_ref=row_recv.at[phase, c, way, pl.ds(PAD, IC * ND)],
             send_sem=send_sem.at[phase, c, way],
             recv_sem=recv_sem.at[phase, c, way],
             device_id={"strip": s + 1 if way == 0 else s - 1},
@@ -73,6 +72,9 @@
         )
 
     def send(phase, c):
+        cols_to(phase, c, 0).start()
+        cols_to(phase, c, 1).start()
+
         @pl.when(has_north)
         def _():
             rows_to(phase, c, 0).start()
@@ -80,9 +82,6 @@
         @pl.when(has_south)
         def _():
             rows_to(phase, c, 1).start()
-
-        cols_to(phase, c, 0).start()
-        cols_to(phase, c, 1).start()
 
     def receive(phase, c):
         cols_to(phase, c, 0).wait_recv()
@@ -106,152 +105,154 @@
         load(c).start()
     for small in smalls:
         small.start()
+
+    barrier = pltpu.get_barrier_semaphore()
+    for side in (east, west):
+        pl.semaphore_signal(barrier, inc=1, device_id={"pt": side}, device_id_type=MESH)
+
+    @pl.when(has_north)
+    def _():
+        pl.semaphore_signal(barrier, inc=1, device_id={"strip": s + 1}, device_id_type=MESH)
+
+    @pl.when(has_south)
+    def _():
+        pl.semaphore_signal(barrier, inc=1, device_id={"strip": s - 1}, device_id_type=MESH)
+
+    @pl.when(jnp.logical_not(has_south))
+    def _():
+        row_recv[:, :, 0] = jnp.zeros(row_recv.shape[:2] + row_recv.shape[3:], jnp.float32)
+
+    @pl.when(jnp.logical_not(has_north))
+    def _():
+        row_recv[:, :, 1] = jnp.zeros(row_recv.shape[:2] + row_recv.shape[3:], jnp.float32)
+
     for i in range(NF):
         table[0, i] = float(WEIGHT[i])
         table[1, i] = float(WEIGHT[i] * RATIO[i])
-
-    barrier = pltpu.get_barrier_semaphore()
-    for side in (east, west):
-        pl.semaphore_signal(barrier, inc=1, device_id={"pt": side}, device_id_type=MESH)
-
-    @pl.when(has_north)
-    def _():
-        pl.semaphore_signal(barrier, inc=1, device_id={"strip": s + 1}, device_id_type=MESH)
-
-    @pl.when(has_south)
-    def _():
-        pl.semaphore_signal(barrier, inc=1, device_id={"strip": s - 1}, device_id_type=MESH)
-
-    @pl.when(jnp.logical_not(has_south))
-    def _():
-        row_recv[:, :, 0] = jnp.zeros(row_recv.shape[:2] + row_recv.shape[3:], jnp.float32)
-
-    @pl.when(jnp.logical_not(has_north))
-    def _():
-        row_recv[:, :, 1] = jnp.zeros(row_recv.shape[:2] + row_recv.shape[3:], jnp.float32)
-
+    blank = jnp.zeros((PAD, 128), jnp.float32)
+    for buffer in (e0, e1):
+        buffer[pl.ds(0, PAD), :] = blank
+        buffer[pl.ds(buffer.shape[0] - PAD, PAD), :] = blank
     lane = lax.broadcasted_iota(jnp.int32, (8, 128), 1)
     sub = lax.broadcasted_iota(jnp.int32, (8, 128), 0)
     low = sub < 4
     first_lane = lane == 0
     last_lane = lane == 127
+    spot = jnp.where(low, lane - 1, lane)
+    row = lax.rem(sub, 4)
+    row_is = [row == j for j in range(4)]
+
+    def base_of(c):
+        return pl.multiple_of(c * RPC, 8) + PAD
 
     def pack_rows(src, phase, c):
-        def one(il, carry):
-            base = pl.multiple_of((c * IC + il) * RPI, 8)
-            to = pl.multiple_of(il * ND, 8)
-            for tile, first, count, at in pieces():
-                up = src[pl.ds(base + first * 8 + 3 + 4 * tile, count, stride=8), :]
-                row_send[phase, c, 0, pl.ds(to + at, count), :] = up
-                down = src[pl.ds(base + (HALF + first) * 8 + 4 * tile, count, stride=8), :]
-                row_send[phase, c, 1, pl.ds(to + at, count), :] = down
-            return carry
-
-        lax.fori_loop(0, IC, one, 0, unroll=True)
-
-    def put(acc, m, rolled_pos, neg):
-        mixed = jnp.where(low, neg, rolled_pos)
-        if m:
-            mixed = pltpu.roll(mixed, m, 1)
-        return jnp.where(lane == m, mixed, acc)
-
+        base = base_of(c)
+        for il in range(IC):
+            for way in range(2):
+                for g in range(HALF // 4):
+                    at = base + il * RPI + (HALF * way + 4 * g) * 8
+                    edge = 3 - 3 * way
+                    parts = [src[pl.ds(at + 8 * j + edge - j, 8), :] for j in range(4)]
+                    packed = parts[0]
+                    for j in range(1, 4):
+                        packed = jnp.where(row_is[j], parts[j], packed)
+                    row_send[phase, c, way, pl.ds(il * ND + 8 * g, 8), :] = packed
+
+    def put(acc, n, pos, neg):
+        mixed = jnp.where(low, neg, pos)
+        return jnp.where(spot == n, pltpu.roll(mixed, n + 1, 1), acc)
+
+    def pack_cols(src, phase, c):
+        base = base_of(c)
+        acc = jnp.zeros((8, 128), jnp.float32)
+        for il in range(IC):
+            for m in range(HALF):
+                pos = src[pl.ds(base + il * RPI + 8 * FROM_WEST[m], 8), :]
+                neg = src[pl.ds(base + il * RPI + 8 * FROM_EAST[m], 8), :]
+                acc = put(acc, il * HALF + m, pos, neg)
+        col_send[phase, c] = acc
+
+    load(0).wait()
+    pack_cols(e0, 0, 0)
+    pack_rows(e0, 0, 0)
     pl.semaphore_wait(
         barrier, 2 + has_north.astype(jnp.int32) + has_south.astype(jnp.int32)
     )
+    send(0, 0)
 
     def first_halo(c, carry):
         load(c).wait()
+        pack_cols(e0, 0, c)
         pack_rows(e0, 0, c)
-
-        def one(il, acc):
-            base = pl.multiple_of((c * IC + il) * RPI, 8)
-            own = jnp.zeros((8, 128), jnp.float32)
-            for m in range(HALF):
-                pos = e0[pl.ds(base + 8 * FROM_WEST[m], 8), :]
-                neg = e0[pl.ds(base + 8 * FROM_EAST[m], 8), :]
-                own = put(own, m, pltpu.roll(pos, 1, 1), neg)
-            return jnp.where(lane < HALF, own, pltpu.roll(acc, HALF, 1))
-
-        col_send[0, c] = lax.fori_loop(
-            0, IC, one, jnp.zeros((8, 128), jnp.float32), unroll=True
-        )
         send(0, c)
         return carry
 
-    lax.fori_loop(0, CH, first_halo, 0)
-
+    lax.fori_loop(1, CH, first_halo, 0)
     for small in smalls:
         small.wait()
     sea = sea_mask[...].astype(jnp.float32)
 
     def advance(src, dst, phase, c, sums):
         receive(phase, c)
+        base = base_of(c)
+        m0, m1 = sums
         halo = pltpu.roll(jnp.where(low, col_recv[phase, c, 1], col_recv[phase, c, 0]), 4, 0)
-        halo = pltpu.roll(halo, 128 - (IC - 1) * HALF, 1)
-
-        def one(il, carry):
-            halo, acc, m0, m1 = carry
+        acc = jnp.zeros((8, 128), jnp.float32)
+        for il in range(IC):
             i = c * IC + il
-            base = pl.multiple_of(i * RPI, 8)
-            at = pl.multiple_of(il * ND, 8)
             speed = courant[i] * sea
             keep = [sea - speed * float(k) for k in (np.abs(COS[:4]) + np.abs(SIN[:4]))]
-            own = jnp.zeros((8, 128), jnp.float32)
             total = jnp.zeros((8, 128), jnp.float32)
 
             def step(d, core, side):
-                if d < HALF:
-                    near = pltpu.roll(core, 1, 0)
-                    r0, r1, way, m = 0, 4, 0, d
-                else:
-                    near = pltpu.roll(core, 7, 0)
-                    r0, r1, way, m = 3, 7, 1, d - HALF
-                h0 = row_recv[phase, c, way, pl.ds(at + m, 1), :]
-                h1 = row_recv[phase, c, way, pl.ds(at + HALF + m, 1), :]
-                near = jnp.where(sub == r0, h0, jnp.where(sub == r1, h1, near))
+                at = base + il * RPI + 8 * d
+                way, m = d // HALF, d % HALF
+                edge = 3 * way
+                near = src[pl.ds(at - 1 + 2 * way, 8), :]
+                beyond = row_recv[
+                    phase, c, way, pl.ds(PAD + il * ND + m // 4 * 8 + m % 4 - edge, 8), :
+                ]
+                near = jnp.where(row_is[edge], beyond, near)
                 flow = float(abs(COS[d])) * side + float(abs(SIN[d])) * near
                 q = d % 6
                 fresh = keep[q if q < 4 else 6 - q] * core + speed * flow
-                dst[pl.ds(base + 8 * d, 8), :] = fresh
+                dst[pl.ds(at, 8), :] = fresh
                 return fresh
 
             for m in range(HALF):
-                pos = src[pl.ds(base + 8 * FROM_WEST[m], 8), :]
-                neg = src[pl.ds(base + 8 * FROM_EAST[m], 8), :]
-                edge = jnp.broadcast_to(halo[:, m : m + 1], (8, 128))
-                rolled_pos = pltpu.roll(pos, 1, 1)
-                rolled_neg = pltpu.roll(neg, 127, 1)
-                swap = pltpu.roll(jnp.where(first_lane, rolled_pos, rolled_neg), 4, 0)
-                side_pos = jnp.where(first_lane, jnp.where(low, edge, swap), rolled_pos)
-                side_neg = jnp.where(last_lane, jnp.where(low, swap, edge), rolled_neg)
+                n = il * HALF + m
+                at_pos = base + il * RPI + 8 * FROM_WEST[m]
+                at_neg = base + il * RPI + 8 * FROM_EAST[m]
+                pos = src[pl.ds(at_pos, 8), :]
+                neg = src[pl.ds(at_neg, 8), :]
+                edge = pltpu.roll(halo, 127 - n, 1)
+                seam_pos = jnp.where(low, edge, src[pl.ds(at_pos - 4, 8), :])
+                seam_neg = jnp.where(low, src[pl.ds(at_neg + 4, 8), :], edge)
+                side_pos = pltpu.roll(jnp.where(last_lane, seam_pos, pos), 1, 1)
+                side_neg = pltpu.roll(jnp.where(first_lane, seam_neg, neg), 127, 1)
                 new_pos = step(FROM_WEST[m], pos, side_pos)
                 new_neg = step(FROM_EAST[m], neg, side_neg)
                 if phase == 0:
-                    own = put(own, m, pltpu.roll(new_pos, 1, 1), new_neg)
+                    acc = put(acc, n, new_pos, new_neg)
                 else:
                     total = total + (new_pos + new_neg)
-            if phase == 0:
-                acc = jnp.where(lane < HALF, own, pltpu.roll(acc, HALF, 1))
-            else:
+            if phase == 1:
                 m0 = m0 + table[0, i] * total
                 m1 = m1 + table[1, i] * total
-            return pltpu.roll(halo, HALF, 1), acc, m0, m1
-
-        zero = jnp.zeros((8, 128), jnp.float32)
-        _, acc, m0, m1 = lax.fori_loop(0, IC, one, (halo, zero) + sums, unroll=True)
         if phase == 0:
             col_send[1, c] = acc
-            pack_rows(dst, 1, c)
-            send(1, c)
         return m0, m1
 
     zero = jnp.zeros((8, 128), jnp.float32)
 
     def first_step(c, carry):
         advance(e0, e1, 0, c, (zero, zero))
+        pack_rows(e1, 1, c)
+        send(1, c)
         return carry
 
     lax.fori_loop(0, CH, first_step, 0)
+
     def second_step(c, sums):
         sums = advance(e1, e0, 1, c, sums)
         store(c).start()
@@ -365,13 +366,13 @@
         in_specs=[hbm] * 3,
         out_specs=[hbm, vmem],
         scratch_shapes=[
-            pltpu.VMEM((total, 128), jnp.float32),
-            pltpu.VMEM((total, 128), jnp.float32),
+            pltpu.VMEM((total + 2 * PAD, 128), jnp.float32),
+            pltpu.VMEM((total + 2 * PAD, 128), jnp.float32),
             pltpu.VMEM((8, 128), jnp.int32),
             pltpu.SMEM((NF,), jnp.float32),
             pltpu.SMEM((2, NF), jnp.float32),
             pltpu.VMEM((2, CH, 2, rows, 128), jnp.float32),
-            pltpu.VMEM((2, CH, 2, rows, 128), jnp.float32),
+            pltpu.VMEM((2, CH, 2, rows + 2 * PAD, 128), jnp.float32),
             pltpu.VMEM((2, CH, 8, 128), jnp.float32),
             pltpu.VMEM((2, CH, 2, 8, 128), jnp.float32),
             sem((CH,)),

time: 19.7 us -> 22.1 us (1.12)
  Pallas kernels: 19.4 us -> 21.9 us
    pallas_call x1, Pallas kernels: 16.3 us -> 18.9 us  [on_device(): pl.pallas_call(functools.partial(kernel, n_strip, n_pt), out_shape=[whole...]
where the time goes in v4:
time: 22.1 us; the launch traced here: 21.9 us
  Pallas kernels  21.9 us (99%)
    pallas_call x1, Pallas kernels, on_device(): pl.pallas_call(functools.partial(kernel, n_strip, n_pt), out_shape=[whole...  18.9 us
    pallas_call x1, Pallas kernels, on_device(): pl.pallas_call(source_kernel, out_shape=whole, in_specs=[hbm] * 5, out_sp...  3.02 us

profile of v4, /device:TPU:1, one launch (start us, length us, event | category | flops | bytes accessed | tf_op | source)
XLA Modules:
  0.0 21.9 jit_solution(13477271736771689606)
XLA Ops:
  0.0 18.9 %shard_map.64 = (f32[4800,128]{1,0:T(8,128)}, f32[8,128]{1,0:T(8,128)}) custom-call(f32[25]{0:T(128)} %courant_in.1, s32[8,128]{1,0:T(8,128)} %bitcast.31, f32[4800,128]{1,0:T(8,128)} %bitcast.30), custom_call_target="tpu_custom_call" | custom-call | flops 18432000 | bytes 4915200 | tf_op jit(solution)/shard_map/pallas_call | solution.py:363
  18.9 3.0 %shard_map.65 = f32[4800,128]{1,0:T(8,128)} custom-call(f32[8,128]{1,0:T(8,128)} %bitcast.32, f32[8,128]{1,0:T(8,128)} %bitcast.33, s32[8,128]{1,0:T(8,128)} %bitcast.34, f32[8,128]{1,0:T(8,128)} %get-tuple-element.7.mean_ratio_in, f32[4800,128]{1,0:T(8,128)} %get-tuple-element.8.energy), custom_call_target="tpu_custom_call" | custom-call | flops 2457600 | bytes 4915200 | tf_op jit(solution)/shard_map/pallas_call | solution.py:391

commit v5 on v2

v5 whole, which is shorter than its diff:
```python
import functools
import numpy as np
import jax
import jax.numpy as jnp
from jax import lax
from jax.experimental import pallas as pl
from jax.experimental.pallas import tpu as pltpu
from jax.sharding import PartitionSpec as P

NF = 25
ND = 24
HALF = ND // 2
CH = 5
IC = NF // CH
RPI = ND * 8
RPC = RPI * IC
GROUPS = NF // 8
LAST = NF - 1
QUAD = ND // 4
MESH = pl.DeviceIdType.MESH

THETA = (np.float32(2.0 * np.pi) * np.arange(ND, dtype=np.float32) / np.float32(ND)).astype(np.float32)
COS = np.cos(THETA).astype(np.float32)
SIN = np.sin(THETA).astype(np.float32)
RATIO = np.float32(1.1) ** np.arange(NF, dtype=np.float32)
WEIGHT = (RATIO / (ND * np.sum(RATIO, dtype=np.float64))).astype(np.float32)
PAIRS = [(m, QUAD + m, 0) for m in range(QUAD)]
PAIRS += [(3 * QUAD + m, 2 * QUAD + m, 1) for m in range(QUAD)]
LAST_PAIRS = [(0, 1, 0), (3, 2, 1)]


def kernel(
    n_strip, n_pt,
    courant_in, sea_in, spectra,
    out, mean_ratio,
    e0, e1, e2, l0, l1, l2,
    sea_mask, sea, courant, speed, weight, sums,
    halo, last_halo, col_send, col_recv,
    in_sem, out_sem, small_sem, row_send_sem, row_recv_sem, col_send_sem, col_recv_sem,
):
    s = lax.axis_index("strip")
    p = lax.axis_index("pt")
    east = lax.rem(p + 1, n_pt)
    west = lax.rem(p + n_pt - 1, n_pt)
    has_south = s > 0
    has_north = s < n_strip - 1

    def load(i):
        return pltpu.make_async_copy(
            spectra.at[i], e0.at[i // 8, :, :, i % 8, :], in_sem.at[i]
        )

    def load_last(d):
        return pltpu.make_async_copy(
            spectra.at[LAST, d], l0.at[d // QUAD, :, d % QUAD, :], in_sem.at[LAST + d]
        )

    def store(g, j):
        return pltpu.make_async_copy(
            e2.at[g, :, :, j, :], out.at[g * 8 + j], out_sem.at[g * 8 + j]
        )

    def store_last(d):
        return pltpu.make_async_copy(
            l2.at[d // QUAD, :, d % QUAD, :], out.at[LAST, d], out_sem.at[LAST + d]
        )

    def rows_to(phase, c, way, tile):
        edge = 4 * tile + 3 - 3 * way
        if isinstance(c, int) and c == GROUPS:
            held = (l0, l1)[phase]
            source = held.at[pl.ds(2 * way, 2), edge]
            target = last_halo.at[phase, way, tile]
        else:
            held = (e0, e1)[phase]
            source = held.at[c, pl.ds(HALF * way, HALF), edge]
            target = halo.at[phase, c, way, tile]
        return pltpu.make_async_remote_copy(
            src_ref=source,
            dst_ref=target,
            send_sem=row_send_sem.at[phase, c, way, tile],
            recv_sem=row_recv_sem.at[phase, c, way, tile],
            device_id={"strip": s + 1 if way == 0 else s - 1},
            device_id_type=MESH,
        )

    def cols_to(phase, c, way):
        return pltpu.make_async_remote_copy(
            src_ref=col_send.at[phase, c],
            dst_ref=col_recv.at[phase, c, way],
            send_sem=col_send_sem.at[phase, c, way],
            recv_sem=col_recv_sem.at[phase, c, way],
            device_id={"pt": east if way == 0 else west},
            device_id_type=MESH,
        )

    def send_rows(phase, c):
        @pl.when(has_north)
        def _():
            rows_to(phase, c, 0, 0).start()
            rows_to(phase, c, 0, 1).start()

        @pl.when(has_south)
        def _():
            rows_to(phase, c, 1, 0).start()
            rows_to(phase, c, 1, 1).start()

    def send_cols(phase, c):
        cols_to(phase, c, 0).start()
        cols_to(phase, c, 1).start()

    def receive(phase, c):
        cols_to(phase, c, 0).wait_recv()
        cols_to(phase, c, 1).wait_recv()

        @pl.when(has_south)
        def _():
            rows_to(phase, c, 0, 0).wait_recv()
            rows_to(phase, c, 0, 1).wait_recv()

        @pl.when(has_north)
        def _():
            rows_to(phase, c, 1, 0).wait_recv()
            rows_to(phase, c, 1, 1).wait_recv()

    smalls = [
        pltpu.make_async_copy(source, target, small_sem.at[n])
        for n, (source, target) in enumerate(((courant_in, courant), (sea_in, sea_mask)))
    ]
    for i in range(LAST):
        load(i).start()
    for small in smalls:
        small.start()

    barrier = pltpu.get_barrier_semaphore()
    for side in (east, west):
        pl.semaphore_signal(barrier, inc=1, device_id={"pt": side}, device_id_type=MESH)

    @pl.when(has_north)
    def _():
        pl.semaphore_signal(barrier, inc=1, device_id={"strip": s + 1}, device_id_type=MESH)

    @pl.when(has_south)
    def _():
        pl.semaphore_signal(barrier, inc=1, device_id={"strip": s - 1}, device_id_type=MESH)

    zero = jnp.zeros((8, 128), jnp.float32)
    l0[...] = jnp.zeros(l0.shape, jnp.float32)
    for d in range(ND):
        load_last(d).start()

    @pl.when(jnp.logical_not(has_south))
    def _():
        halo[:, :, 0] = jnp.zeros(halo.shape[:2] + halo.shape[3:], jnp.float32)
        last_halo[:, 0] = jnp.zeros(last_halo.shape[:1] + last_halo.shape[2:], jnp.float32)

    @pl.when(jnp.logical_not(has_north))
    def _():
        halo[:, :, 1] = jnp.zeros(halo.shape[:2] + halo.shape[3:], jnp.float32)
        last_halo[:, 1] = jnp.zeros(last_halo.shape[:1] + last_halo.shape[2:], jnp.float32)

    lane = lax.broadcasted_iota(jnp.int32, (8, 128), 1)
    sub = lax.broadcasted_iota(jnp.int32, (8, 128), 0)
    couple = lane // 2
    even = lax.rem(lane, 2) == 0
    first_lane = lane == 0
    last_lane = lane == 127

    def by_sub(values):
        made = zero
        for j, value in enumerate(values):
            made = jnp.where(sub == j, value, made)
        return made

    for small in smalls:
        small.wait()
    for g in range(GROUPS):
        speed[g] = by_sub([courant[8 * g + j] for j in range(8)])
        weight[0, g] = by_sub([float(WEIGHT[8 * g + j]) for j in range(8)])
        weight[1, g] = by_sub([float(WEIGHT[8 * g + j] * RATIO[8 * g + j]) for j in range(8)])
    sea_now = sea_mask[...].astype(jnp.float32)
    for t in range(8):
        sea[t] = jnp.broadcast_to(sea_now[t : t + 1], (8, 128))

    def put(acc, n, pos, neg):
        mixed = pltpu.roll(jnp.where(last_lane, pos, neg), 2 * n + 1, 1)
        return jnp.where(couple == n, mixed, acc)

    def pack_cols(src, pairs):
        acc = zero
        for n, (west_block, east_block, _) in enumerate(pairs):
            for y in range(4):
                acc = put(acc, 4 * n + y, src[west_block, 4 + y], src[east_block, y])
        return acc

    def first_halo(c, carry):
        send_rows(0, c)
        col_send[0, c] = pack_cols(e0.at[c], PAIRS)
        send_cols(0, c)
        return carry

    for j in range(8):
        load(j).wait()
    pl.semaphore_wait(
        barrier, 2 + has_north.astype(jnp.int32) + has_south.astype(jnp.int32)
    )

    def loaded(c, carry):
        @pl.when(c > 0)
        def _():
            for j in range(8):
                pltpu.make_async_copy(
                    spectra.at[c * 8 + j], e0.at[c, :, :, j, :], in_sem.at[c * 8 + j]
                ).wait()

        return first_halo(c, carry)

    lax.fori_loop(0, GROUPS, loaded, 0)
    for d in range(ND):
        load_last(d).wait()
    send_rows(0, GROUPS)
    col_send[0, GROUPS] = pack_cols(l0, LAST_PAIRS)
    send_cols(0, GROUPS)

    def advance(phase, c, src, dst, row_halo, pairs, coefficients):
        edges = jnp.where(even, pltpu.roll(col_recv[phase, c, 0], 2, 1), col_recv[phase, c, 1])
        acc = zero
        totals = [zero] * 8
        for n, (west_block, east_block, way) in enumerate(pairs):
            near_halo = [
                [row_halo[way, t, block - way * (len(pairs))] for t in range(2)]
                for block in (west_block, east_block)
            ]
            cores = [
                [[src[block, 4 * t + y] for t in range(2)] for y in range(4)]
                for block in (west_block, east_block)
            ]
            terms = [coefficients(block) for block in (west_block, east_block)]
            for y in range(4):
                edge = pltpu.roll(edges, 128 - (2 * (4 * n + y) + 2), 1)
                w0, w1 = [pltpu.roll(x, 1, 1) for x in cores[0][y]]
                x0, x1 = [pltpu.roll(x, 127, 1) for x in cores[1][y]]
                sides = (
                    (jnp.where(first_lane, edge, w0), jnp.where(first_lane, w0, w1)),
                    (jnp.where(last_lane, x1, x0), jnp.where(last_lane, edge, x1)),
                )
                back = y - 1 + 2 * way
                fresh = []
                for k, block in enumerate((west_block, east_block)):
                    along, across, keep = terms[k]
                    near = cores[k][back] if 0 <= back < 4 else near_halo[k]
                    for t in range(2):
                        moved = keep * cores[k][y][t] + (along * sides[k][t] + across * near[t])
                        moved = moved * sea[4 * t + y]
                        dst[block, 4 * t + y] = moved
                        fresh.append(moved)
                if phase == 0:
                    acc = put(acc, 4 * n + y, fresh[1], fresh[2])
                else:
                    totals[y] = totals[y] + (fresh[0] + fresh[2])
                    totals[4 + y] = totals[4 + y] + (fresh[1] + fresh[3])
        if phase == 0:
            col_send[1, c] = acc
        return totals

    def group(phase, c):
        now = speed[c]

        def coefficients(d):
            cos, sin = float(abs(COS[d])), float(abs(SIN[d]))
            return cos * now, sin * now, 1.0 - (cos + sin) * now

        src, dst = ((e0, e1), (e1, e2))[phase]
        receive(phase, c)
        return advance(
            phase, c, src.at[c], dst.at[c], halo.at[phase, c], PAIRS, coefficients
        )

    def leftover(phase):
        now = courant[LAST]

        def coefficients(q):
            cos = by_sub([float(abs(COS[QUAD * q + j])) for j in range(QUAD)])
            sin = by_sub([float(abs(SIN[QUAD * q + j])) for j in range(QUAD)])
            return cos * now, sin * now, 1.0 - (cos + sin) * now

        src, dst = ((l0, l1), (l1, l2))[phase]
        receive(phase, GROUPS)
        return advance(
            phase, GROUPS, src, dst, last_halo.at[phase], LAST_PAIRS, coefficients
        )

    def first_step(c, carry):
        group(0, c)
        send_cols(1, c)
        send_rows(1, c)
        return carry

    lax.fori_loop(0, GROUPS, first_step, 0)
    leftover(0)
    send_cols(1, GROUPS)
    send_rows(1, GROUPS)

    sums[...] = jnp.zeros(sums.shape, jnp.float32)

    def second_step(c, carry):
        totals = group(1, c)
        for j in range(8):
            store(c, j).start()
        for t in range(8):
            sums[0, t] = sums[0, t] + weight[0, c] * totals[t]
            sums[1, t] = sums[1, t] + weight[1, c] * totals[t]
        return carry

    lax.fori_loop(0, GROUPS, second_step, 0)
    totals = leftover(1)
    for d in range(ND):
        store_last(d).start()
    for t in range(8):
        rest = jnp.where(sub < QUAD, totals[t], 0.0)
        m0 = sums[0, t] + float(WEIGHT[LAST]) * rest
        m1 = sums[1, t] + float(WEIGHT[LAST] * RATIO[LAST]) * rest
        m0 = jnp.sum(m0, axis=0, keepdims=True)
        m1 = jnp.sum(m1, axis=0, keepdims=True)
        mean_ratio[pl.ds(t, 1), :] = m1 / jnp.maximum(m0, 0.05)

    for phase in range(2):
        for c in range(GROUPS + 1):
            @pl.when(has_north)
            def _():
                rows_to(phase, c, 0, 0).wait_send()
                rows_to(phase, c, 0, 1).wait_send()

            @pl.when(has_south)
            def _():
                rows_to(phase, c, 1, 0).wait_send()
                rows_to(phase, c, 1, 1).wait_send()

            cols_to(phase, c, 0).wait_send()
            cols_to(phase, c, 1).wait_send()
    for i in range(LAST):
        store(i // 8, i % 8).wait()
    for d in range(ND):
        store_last(d).wait()


def source_kernel(
    wind_speed_in, wind_dir_in, ice_in, mean_ratio_in, energy,
    out,
    held, done, wind_speed, wind_dir, ice_mask, mean_ratio, gain,
    in_sem, out_sem, small_sem,
):
    loads = [
        pltpu.make_async_copy(
            energy.at[pl.ds(c * RPC, RPC), :], held.at[pl.ds(c * RPC, RPC), :], in_sem.at[c]
        )
        for c in range(CH)
    ]
    stores = [
        pltpu.make_async_copy(
            done.at[pl.ds(c * RPC, RPC), :], out.at[pl.ds(c * RPC, RPC), :], out_sem.at[c]
        )
        for c in range(CH)
    ]
    smalls = [
        pltpu.make_async_copy(source, target, small_sem.at[n])
        for n, (source, target) in enumerate(
            (
                (wind_dir_in, wind_dir),
                (wind_speed_in, wind_speed),
                (ice_in, ice_mask),
                (mean_ratio_in, mean_ratio),
            )
        )
    ]
    for copy in smalls + loads:
        copy.start()
    for copy in smalls:
        copy.wait()
    ice = ice_mask[...].astype(jnp.float32)
    strength = (1.0 - ice) * 0.05 * wind_speed[...]
    cos_wind = strength * jnp.cos(wind_dir[...])
    sin_wind = strength * jnp.sin(wind_dir[...])
    for d in range(ND):
        gain[pl.ds(8 * d, 8), :] = jnp.maximum(
            float(COS[d]) * cos_wind + float(SIN[d]) * sin_wind, 0.0
        )
    drag = 0.02 * mean_ratio[...]
    cold = 0.7 * ice
    for c in range(CH):
        loads[c].wait()
        losses = [float(RATIO[c * IC + il]) * drag + cold for il in range(IC)]

        def one(d, carry):
            push = gain[pl.ds(pl.multiple_of(8 * d, 8), 8), :]
            for il in range(IC):
                rows = pl.ds(pl.multiple_of((c * IC + il) * RPI + 8 * d, 8), 8)
                net = float(RATIO[c * IC + il]) * push - losses[il]
                done[rows, :] = held[rows, :] * jnp.exp(net)
            return carry

        lax.fori_loop(0, ND, one, 0, unroll=8)
        stores[c].start()
    for copy in stores:
        copy.wait()


def to_tiles(x):
    lead, rows, cols = x.shape
    x = x.reshape(lead, rows, cols // 128, 128).transpose(0, 2, 1, 3)
    return x.reshape(lead * rows * cols // 128, 128)


def from_tiles(x, shape):
    lead, rows, cols = shape
    x = x.reshape(lead, cols // 128, rows, 128).transpose(0, 2, 1, 3)
    return x.reshape(shape)


def on_device(n_strip, n_pt, spectra, courant, wind_speed, wind_dir, sea_mask, ice_mask):
    total = spectra.shape[0] * 8
    vmem = pl.BlockSpec(memory_space=pltpu.VMEM)
    hbm = pl.BlockSpec(memory_space=pl.ANY)
    sem = pltpu.SemaphoreType.DMA
    whole = jax.ShapeDtypeStruct((total, 128), jnp.float32)
    tiles = (NF, ND, 8, 128)
    blocks = pltpu.VMEM((GROUPS, ND, 8, 8, 128), jnp.float32)
    last_blocks = pltpu.VMEM((4, 8, 8, 128), jnp.float32)
    energy, mean_ratio = pl.pallas_call(
        functools.partial(kernel, n_strip, n_pt),
        out_shape=[
            jax.ShapeDtypeStruct(tiles, jnp.float32),
            jax.ShapeDtypeStruct((8, 128), jnp.float32),
        ],
        in_specs=[hbm] * 3,
        out_specs=[hbm, vmem],
        scratch_shapes=[
            blocks,
            blocks,
            blocks,
            last_blocks,
            last_blocks,
            last_blocks,
            pltpu.VMEM((8, 128), jnp.int32),
            pltpu.VMEM((8, 8, 128), jnp.float32),
            pltpu.SMEM((NF,), jnp.float32),
            pltpu.VMEM((GROUPS, 8, 128), jnp.float32),
            pltpu.VMEM((2, GROUPS, 8, 128), jnp.float32),
            pltpu.VMEM((2, 8, 8, 128), jnp.float32),
            pltpu.VMEM((2, GROUPS, 2, 2, HALF, 8, 128), jnp.float32),
            pltpu.VMEM((2, 2, 2, 2, 8, 128), jnp.float32),
            pltpu.VMEM((2, GROUPS + 1, 8, 128), jnp.float32),
            pltpu.VMEM((2, GROUPS + 1, 2, 8, 128), jnp.float32),
            sem((LAST + ND,)),
            sem((LAST + ND,)),
            sem((2,)),
            sem((2, GROUPS + 1, 2, 2)),
            sem((2, GROUPS + 1, 2, 2)),
            sem((2, GROUPS + 1, 2)),
            sem((2, GROUPS + 1, 2)),
        ],
        compiler_params=pltpu.CompilerParams(
            collective_id=0, has_side_effects=True, vmem_limit_bytes=60 * 1024 * 1024
        ),
        cost_estimate=pl.CostEstimate(
            flops=16 * total * 128, bytes_accessed=8 * total * 128, transcendentals=0
        ),
    )(courant, to_tiles(sea_mask[None]), to_tiles(spectra).reshape(tiles))
    result = pl.pallas_call(
        source_kernel,
        out_shape=whole,
        in_specs=[hbm] * 5,
        out_specs=hbm,
        scratch_shapes=[
            pltpu.VMEM((total, 128), jnp.float32),
            pltpu.VMEM((total, 128), jnp.float32),
            pltpu.VMEM((8, 128), jnp.float32),
            pltpu.VMEM((8, 128), jnp.float32),
            pltpu.VMEM((8, 128), jnp.int32),
            pltpu.VMEM((8, 128), jnp.float32),
            pltpu.VMEM((ND * 8, 128), jnp.float32),
            sem((CH,)),
            sem((CH,)),
            sem((4,)),
        ],
        compiler_params=pltpu.CompilerParams(vmem_limit_bytes=60 * 1024 * 1024),
        cost_estimate=pl.CostEstimate(
            flops=4 * total * 128, bytes_accessed=8 * total * 128, transcendentals=total * 128
        ),
    )(
        to_tiles(wind_speed[None]),
        to_tiles(wind_dir[None]),
        to_tiles(ice_mask[None]),
        mean_ratio,
        energy.reshape(total, 128),
    )
    return from_tiles(result, spectra.shape)


def solution(mesh):
    in_specs = (
        P(None, "strip", "pt"),
        P(),
        P("strip", "pt"),
        P("strip", "pt"),
        P("strip", "pt"),
        P("strip", "pt"),
    )
    return jax.shard_map(
        functools.partial(on_device, mesh.shape["strip"], mesh.shape["pt"]),
        mesh=mesh,
        in_specs=in_specs,
        out_specs=P(None, "strip", "pt"),
        check_vma=False,
    )
```

time: 19.7 us -> 23.9 us (1.21)
  Pallas kernels: 19.4 us -> 23.7 us
    pallas_call x1, Pallas kernels: 16.3 us -> 20.7 us  [on_device(): pl.pallas_call(functools.partial(kernel, n_strip, n_pt), out_shape=[jax.S...]
where the time goes in v5:
time: 23.9 us; the launch traced here: 23.7 us
  Pallas kernels  23.7 us (99%)
    pallas_call x1, Pallas kernels, on_device(): pl.pallas_call(functools.partial(kernel, n_strip, n_pt), out_shape=[jax.S...  20.7 us
    pallas_call x1, Pallas kernels, on_device(): pl.pallas_call(source_kernel, out_shape=whole, in_specs=[hbm] * 5, out_sp...  3.02 us

profile of v5, /device:TPU:1, one launch (start us, length us, event | category | flops | bytes accessed | tf_op | source)
XLA Modules:
  0.0 23.7 jit_solution(16133887087461797898)
XLA Ops:
  0.0 20.7 %shard_map.64 = (f32[25,24,8,128]{3,2,1,0:T(8,128)}, f32[8,128]{1,0:T(8,128)}) custom-call(f32[25]{0:T(128)} %courant_in.1, s32[8,128]{1,0:T(8,128)} %bitcast.33, f32[25,24,8,128]{3,2,1,0:T(8,128)} %bitcast.31), custom_call_target="tpu_custom_call" | custom-call | flops 9830400 | bytes 4915200 | tf_op jit(solution)/shard_map/pallas_call | solution.py:429
  20.7 3.0 %shard_map.65 = f32[4800,128]{1,0:T(8,128)} custom-call(f32[8,128]{1,0:T(8,128)} %bitcast.34, f32[8,128]{1,0:T(8,128)} %bitcast.35, s32[8,128]{1,0:T(8,128)} %bitcast.36, f32[8,128]{1,0:T(8,128)} %get-tuple-element.7.mean_ratio_in, f32[4800,128]{1,0:T(8,128)} %bitcast.32), custom_call_target="tpu_custom_call" | custom-call | flops 2457600 | bytes 4915200 | tf_op jit(solution)/shard_map/pallas_call | solution.py:469

commit v6 on v5

--- a/solution.py
+++ b/solution.py
@@ -14,6 +14,7 @@
 IC = NF // CH
 RPI = ND * 8
 RPC = RPI * IC
+RPG = RPI * 8
 GROUPS = NF // 8
 LAST = NF - 1
 QUAD = ND // 4
@@ -33,7 +34,7 @@
     n_strip, n_pt,
     courant_in, sea_in, spectra,
     out, mean_ratio,
-    e0, e1, e2, l0, l1, l2,
+    raw, done, e0, e1, l0, l1,
     sea_mask, sea, courant, speed, weight, sums,
     halo, last_halo, col_send, col_recv,
     in_sem, out_sem, small_sem, row_send_sem, row_recv_sem, col_send_sem, col_recv_sem,
@@ -45,25 +46,13 @@
     has_south = s > 0
     has_north = s < n_strip - 1
 
-    def load(i):
-        return pltpu.make_async_copy(
-            spectra.at[i], e0.at[i // 8, :, :, i % 8, :], in_sem.at[i]
-        )
-
-    def load_last(d):
-        return pltpu.make_async_copy(
-            spectra.at[LAST, d], l0.at[d // QUAD, :, d % QUAD, :], in_sem.at[LAST + d]
-        )
-
-    def store(g, j):
-        return pltpu.make_async_copy(
-            e2.at[g, :, :, j, :], out.at[g * 8 + j], out_sem.at[g * 8 + j]
-        )
-
-    def store_last(d):
-        return pltpu.make_async_copy(
-            l2.at[d // QUAD, :, d % QUAD, :], out.at[LAST, d], out_sem.at[LAST + d]
-        )
+    def load(c):
+        rows = pl.ds(c * RPG, RPI if isinstance(c, int) and c == GROUPS else RPG)
+        return pltpu.make_async_copy(spectra.at[rows, :], raw.at[rows, :], in_sem.at[c])
+
+    def store(c):
+        rows = pl.ds(c * RPG, RPI if isinstance(c, int) and c == GROUPS else RPG)
+        return pltpu.make_async_copy(done.at[rows, :], out.at[rows, :], out_sem.at[c])
 
     def rows_to(phase, c, way, tile):
         edge = 4 * tile + 3 - 3 * way
@@ -127,8 +116,8 @@
         pltpu.make_async_copy(source, target, small_sem.at[n])
         for n, (source, target) in enumerate(((courant_in, courant), (sea_in, sea_mask)))
     ]
-    for i in range(LAST):
-        load(i).start()
+    for c in range(GROUPS + 1):
+        load(c).start()
     for small in smalls:
         small.start()
 
@@ -145,9 +134,7 @@
         pl.semaphore_signal(barrier, inc=1, device_id={"strip": s - 1}, device_id_type=MESH)
 
     zero = jnp.zeros((8, 128), jnp.float32)
-    l0[...] = jnp.zeros(l0.shape, jnp.float32)
-    for d in range(ND):
-        load_last(d).start()
+    raw[pl.ds(NF * RPI, 16), :] = jnp.zeros((16, 128), jnp.float32)
 
     @pl.when(jnp.logical_not(has_south))
     def _():
@@ -193,36 +180,40 @@
                 acc = put(acc, 4 * n + y, src[west_block, 4 + y], src[east_block, y])
         return acc
 
+    pl.semaphore_wait(
+        barrier, 2 + has_north.astype(jnp.int32) + has_south.astype(jnp.int32)
+    )
+
+    def gather(c, d, t):
+        start = pl.multiple_of(c * RPG, 8) + d * 8 + t
+        e0[c, d, t] = raw[pl.ds(start, 8, stride=RPI), :]
+
     def first_halo(c, carry):
+        pltpu.make_async_copy(
+            spectra.at[pl.ds(c * RPG, RPG), :], raw.at[pl.ds(c * RPG, RPG), :], in_sem.at[c]
+        ).wait()
+        outer = [(d, t) for d in range(ND) for t in ((3, 7) if d < HALF else (0, 4))]
+        for d, t in outer:
+            gather(c, d, t)
         send_rows(0, c)
+        for d in range(ND):
+            for t in range(8):
+                if (d, t) not in outer:
+                    gather(c, d, t)
         col_send[0, c] = pack_cols(e0.at[c], PAIRS)
         send_cols(0, c)
         return carry
 
-    for j in range(8):
-        load(j).wait()
-    pl.semaphore_wait(
-        barrier, 2 + has_north.astype(jnp.int32) + has_south.astype(jnp.int32)
-    )
-
-    def loaded(c, carry):
-        @pl.when(c > 0)
-        def _():
-            for j in range(8):
-                pltpu.make_async_copy(
-                    spectra.at[c * 8 + j], e0.at[c, :, :, j, :], in_sem.at[c * 8 + j]
-                ).wait()
-
-        return first_halo(c, carry)
-
-    lax.fori_loop(0, GROUPS, loaded, 0)
-    for d in range(ND):
-        load_last(d).wait()
+    lax.fori_loop(0, GROUPS, first_halo, 0)
+    load(GROUPS).wait()
+    for q in range(4):
+        for t in range(8):
+            l0[q, t] = raw[pl.ds(LAST * RPI + q * QUAD * 8 + t, 8, stride=8), :]
     send_rows(0, GROUPS)
     col_send[0, GROUPS] = pack_cols(l0, LAST_PAIRS)
     send_cols(0, GROUPS)
 
-    def advance(phase, c, src, dst, row_halo, pairs, coefficients):
+    def advance(phase, c, src, write, row_halo, pairs, coefficients):
         edges = jnp.where(even, pltpu.roll(col_recv[phase, c, 0], 2, 1), col_recv[phase, c, 1])
         acc = zero
         totals = [zero] * 8
@@ -252,7 +243,7 @@
                     for t in range(2):
                         moved = keep * cores[k][y][t] + (along * sides[k][t] + across * near[t])
                         moved = moved * sea[4 * t + y]
-                        dst[block, 4 * t + y] = moved
+                        write(block, 4 * t + y, moved)
                         fresh.append(moved)
                 if phase == 0:
                     acc = put(acc, 4 * n + y, fresh[1], fresh[2])
@@ -270,10 +261,17 @@
             cos, sin = float(abs(COS[d])), float(abs(SIN[d]))
             return cos * now, sin * now, 1.0 - (cos + sin) * now
 
-        src, dst = ((e0, e1), (e1, e2))[phase]
+        def write(d, t, value):
+            if phase == 0:
+                e1[c, d, t] = value
+            else:
+                start = pl.multiple_of(c * RPG, 8) + d * 8 + t
+                done[pl.ds(start, 8, stride=RPI), :] = value
+
+        src = (e0, e1)[phase]
         receive(phase, c)
         return advance(
-            phase, c, src.at[c], dst.at[c], halo.at[phase, c], PAIRS, coefficients
+            phase, c, src.at[c], write, halo.at[phase, c], PAIRS, coefficients
         )
 
     def leftover(phase):
@@ -284,10 +282,17 @@
             sin = by_sub([float(abs(SIN[QUAD * q + j])) for j in range(QUAD)])
             return cos * now, sin * now, 1.0 - (cos + sin) * now
 
-        src, dst = ((l0, l1), (l1, l2))[phase]
+        def write(q, t, value):
+            if phase == 0:
+                l1[q, t] = value
+            else:
+                rows = pl.ds(LAST * RPI + q * QUAD * 8 + t, QUAD, stride=8)
+                done[rows, :] = value[:QUAD]
+
+        src = (l0, l1)[phase]
         receive(phase, GROUPS)
         return advance(
-            phase, GROUPS, src, dst, last_halo.at[phase], LAST_PAIRS, coefficients
+            phase, GROUPS, src, write, last_halo.at[phase], LAST_PAIRS, coefficients
         )
 
     def first_step(c, carry):
@@ -305,8 +310,9 @@
 
     def second_step(c, carry):
         totals = group(1, c)
-        for j in range(8):
-            store(c, j).start()
+        pltpu.make_async_copy(
+            done.at[pl.ds(c * RPG, RPG), :], out.at[pl.ds(c * RPG, RPG), :], out_sem.at[c]
+        ).start()
         for t in range(8):
             sums[0, t] = sums[0, t] + weight[0, c] * totals[t]
             sums[1, t] = sums[1, t] + weight[1, c] * totals[t]
@@ -314,8 +320,7 @@
 
     lax.fori_loop(0, GROUPS, second_step, 0)
     totals = leftover(1)
-    for d in range(ND):
-        store_last(d).start()
+    store(GROUPS).start()
     for t in range(8):
         rest = jnp.where(sub < QUAD, totals[t], 0.0)
         m0 = sums[0, t] + float(WEIGHT[LAST]) * rest
@@ -338,10 +343,8 @@
 
             cols_to(phase, c, 0).wait_send()
             cols_to(phase, c, 1).wait_send()
-    for i in range(LAST):
-        store(i // 8, i % 8).wait()
-    for d in range(ND):
-        store_last(d).wait()
+    for c in range(GROUPS + 1):
+        store(c).wait()
 
 
 def source_kernel(
@@ -423,22 +426,21 @@
     hbm = pl.BlockSpec(memory_space=pl.ANY)
     sem = pltpu.SemaphoreType.DMA
     whole = jax.ShapeDtypeStruct((total, 128), jnp.float32)
-    tiles = (NF, ND, 8, 128)
     blocks = pltpu.VMEM((GROUPS, ND, 8, 8, 128), jnp.float32)
     last_blocks = pltpu.VMEM((4, 8, 8, 128), jnp.float32)
     energy, mean_ratio = pl.pallas_call(
         functools.partial(kernel, n_strip, n_pt),
         out_shape=[
-            jax.ShapeDtypeStruct(tiles, jnp.float32),
+            whole,
             jax.ShapeDtypeStruct((8, 128), jnp.float32),
         ],
         in_specs=[hbm] * 3,
         out_specs=[hbm, vmem],
         scratch_shapes=[
+            pltpu.VMEM((total + 16, 128), jnp.float32),
+            pltpu.VMEM((total, 128), jnp.float32),
             blocks,
             blocks,
-            blocks,
-            last_blocks,
             last_blocks,
             last_blocks,
             pltpu.VMEM((8, 128), jnp.int32),
@@ -451,8 +453,8 @@
             pltpu.VMEM((2, 2, 2, 2, 8, 128), jnp.float32),
             pltpu.VMEM((2, GROUPS + 1, 8, 128), jnp.float32),
             pltpu.VMEM((2, GROUPS + 1, 2, 8, 128), jnp.float32),
-            sem((LAST + ND,)),
-            sem((LAST + ND,)),
+            sem((GROUPS + 1,)),
+            sem((GROUPS + 1,)),
             sem((2,)),
             sem((2, GROUPS + 1, 2, 2)),
             sem((2, GROUPS + 1, 2, 2)),
@@ -465,7 +467,7 @@
         cost_estimate=pl.CostEstimate(
             flops=16 * total * 128, bytes_accessed=8 * total * 128, transcendentals=0
         ),
-    )(courant, to_tiles(sea_mask[None]), to_tiles(spectra).reshape(tiles))
+    )(courant, to_tiles(sea_mask[None]), to_tiles(spectra))
     result = pl.pallas_call(
         source_kernel,
         out_shape=whole,
@@ -492,7 +494,7 @@
         to_tiles(wind_dir[None]),
         to_tiles(ice_mask[None]),
         mean_ratio,
-        energy.reshape(total, 128),
+        energy,
     )
     return from_tiles(result, spectra.shape)
 

time: 23.9 us -> 23.6 us (0.987)
  Pallas kernels: 23.7 us -> 23.4 us
    pallas_call x1, Pallas kernels: 20.7 us -> 20.4 us  [on_device(): pl.pallas_call(functools.partial(kernel, n_strip, n_pt), out_shape=[whole...]
where the time goes in v6:
time: 23.6 us; the launch traced here: 23.4 us
  Pallas kernels  23.4 us (99%)
    pallas_call x1, Pallas kernels, on_device(): pl.pallas_call(functools.partial(kernel, n_strip, n_pt), out_shape=[whole...  20.4 us
    pallas_call x1, Pallas kernels, on_device(): pl.pallas_call(source_kernel, out_shape=whole, in_specs=[hbm] * 5, out_sp...  3.02 us

profile of v6, /device:TPU:1, one launch (start us, length us, event | category | flops | bytes accessed | tf_op | source)
XLA Modules:
  0.0 23.4 jit_solution(5780381815248164628)
XLA Ops:
  0.0 20.4 %shard_map.64 = (f32[4800,128]{1,0:T(8,128)}, f32[8,128]{1,0:T(8,128)}) custom-call(f32[25]{0:T(128)} %courant_in.1, s32[8,128]{1,0:T(8,128)} %bitcast.31, f32[4800,128]{1,0:T(8,128)} %bitcast.30), custom_call_target="tpu_custom_call" | custom-call | flops 9830400 | bytes 4915200 | tf_op jit(solution)/shard_map/pallas_call | solution.py:431
  20.4 3.0 %shard_map.65 = f32[4800,128]{1,0:T(8,128)} custom-call(f32[8,128]{1,0:T(8,128)} %bitcast.32, f32[8,128]{1,0:T(8,128)} %bitcast.33, s32[8,128]{1,0:T(8,128)} %bitcast.34, f32[8,128]{1,0:T(8,128)} %get-tuple-element.7.mean_ratio_in, f32[4800,128]{1,0:T(8,128)} %get-tuple-element.8.energy), custom_call_target="tpu_custom_call" | custom-call | flops 2457600 | bytes 4915200 | tf_op jit(solution)/shard_map/pallas_call | solution.py:471

commit v7 on v3

--- a/solution.py
+++ b/solution.py
@@ -34,8 +34,8 @@
     courant_in, sea_in, spectra,
     out, mean_ratio,
     e0, e1, sea_mask, sea, courant, table, rise,
-    row_send, row_recv, col_send, col_recv,
-    in_sem, out_sem, small_sem, send_sem, recv_sem,
+    row_send, row_recv, col_send, col_recv, corner_recv, turn,
+    in_sem, out_sem, small_sem, send_sem, recv_sem, corner_send_sem, corner_recv_sem,
 ):
     s = lax.axis_index("strip")
     p = lax.axis_index("pt")
@@ -72,6 +72,34 @@
             device_id_type=MESH,
         )
 
+    def corners_to(c, way):
+        return pltpu.make_async_remote_copy(
+            src_ref=col_send.at[0, c],
+            dst_ref=corner_recv.at[c, way],
+            send_sem=corner_send_sem.at[c, way],
+            recv_sem=corner_recv_sem.at[c, way],
+            device_id={"strip": s + 1 if way == 0 else s - 1},
+            device_id_type=MESH,
+        )
+
+    def send_corners(c):
+        @pl.when(has_north)
+        def _():
+            corners_to(c, 0).start()
+
+        @pl.when(has_south)
+        def _():
+            corners_to(c, 1).start()
+
+    def receive_corners(c):
+        @pl.when(has_south)
+        def _():
+            corners_to(c, 0).wait_recv()
+
+        @pl.when(has_north)
+        def _():
+            corners_to(c, 1).wait_recv()
+
     def send_rows(phase, c):
         @pl.when(has_north)
         def _():
@@ -124,10 +152,12 @@
     @pl.when(jnp.logical_not(has_south))
     def _():
         row_recv[:, :, 0] = jnp.zeros(row_recv.shape[:2] + row_recv.shape[3:], jnp.float32)
+        corner_recv[:, 0] = jnp.zeros((CH, 8, 128), jnp.float32)
 
     @pl.when(jnp.logical_not(has_north))
     def _():
         row_recv[:, :, 1] = jnp.zeros(row_recv.shape[:2] + row_recv.shape[3:], jnp.float32)
+        corner_recv[:, 1] = jnp.zeros((CH, 8, 128), jnp.float32)
 
     for i in range(NF):
         table[0, i] = float(WEIGHT[i])
@@ -154,25 +184,23 @@
 
         lax.fori_loop(0, IC, one, 0, unroll=True)
 
-    def put(acc, m, rolled_pos, neg):
-        mixed = jnp.where(low, neg, rolled_pos)
-        if m:
-            mixed = pltpu.roll(mixed, m, 1)
-        return jnp.where(lane == m, mixed, acc)
+    spot = jnp.where(low, lane - 1, lane)
+    pair = lax.rem(spot, HALF)
+    south = pair < HALF // 2
+
+    def put(acc, n, pos, neg):
+        mixed = pltpu.roll(jnp.where(low, neg, pos), n + 1, 1)
+        return jnp.where(spot == n, mixed, acc)
 
     def pack_cols(src, phase, c):
-        def one(il, acc):
-            base = pl.multiple_of((c * IC + il) * RPI, 8)
-            own = jnp.zeros((8, 128), jnp.float32)
+        base = pl.multiple_of(c * RPC, 8)
+        acc = jnp.zeros((8, 128), jnp.float32)
+        for il in range(IC):
             for m in range(HALF):
-                pos = src[pl.ds(base + 8 * FROM_WEST[m], 8), :]
-                neg = src[pl.ds(base + 8 * FROM_EAST[m], 8), :]
-                own = put(own, m, pltpu.roll(pos, 1, 1), neg)
-            return jnp.where(lane < HALF, own, pltpu.roll(acc, HALF, 1))
-
-        col_send[phase, c] = lax.fori_loop(
-            0, IC, one, jnp.zeros((8, 128), jnp.float32), unroll=True
-        )
+                pos = src[pl.ds(base + il * RPI + 8 * FROM_WEST[m], 8), :]
+                neg = src[pl.ds(base + il * RPI + 8 * FROM_EAST[m], 8), :]
+                acc = put(acc, il * HALF + m, pos, neg)
+        col_send[phase, c] = acc
 
     load(0).wait()
     pack_cols(e0, 0, 0)
@@ -181,12 +209,14 @@
         barrier, 2 + has_north.astype(jnp.int32) + has_south.astype(jnp.int32)
     )
     send_cols(0, 0)
+    send_corners(0)
     send_rows(0, 0)
 
     def first_halo(c, carry):
         load(c).wait()
         pack_cols(e0, 0, c)
         send_cols(0, c)
+        send_corners(c)
         pack_rows(e0, 0, c)
         send_rows(0, c)
         return carry
@@ -194,21 +224,35 @@
     lax.fori_loop(1, CH, first_halo, 0)
     for small in smalls:
         small.wait()
-    sea[...] = sea_mask[...].astype(jnp.float32)
+    sea_all = sea_mask[...].astype(jnp.float32)
+    sea[...] = sea_all
+    slope = jnp.zeros((8, 128), jnp.float32)
+    for m in range(HALF):
+        here = jnp.where(low, float(abs(SIN[FROM_EAST[m]])), float(abs(SIN[FROM_WEST[m]])))
+        slope = jnp.where(pair == m, here, slope)
+    edge_row = lax.rem(sub, 4) == jnp.where(south, 0, 3)
+    used = edge_row & (spot >= 0) & (spot < IC * HALF)
+    shore = jnp.where(
+        low,
+        jnp.broadcast_to(sea_all[:, 0:1], (8, 128)),
+        jnp.broadcast_to(sea_all[:, 127:128], (8, 128)),
+    )
+    turn[...] = jnp.where(used, slope * shore, 0.0)
 
     def advance(src, dst, phase, c, sums):
         receive_cols(phase, c)
         if phase == 1:
             receive_rows(phase, c)
-        halo = pltpu.roll(jnp.where(low, col_recv[phase, c, 1], col_recv[phase, c, 0]), 4, 0)
-        halo = pltpu.roll(halo, 128 - (IC - 1) * HALF, 1)
+        halo = jnp.where(low, col_recv[phase, c, 1], pltpu.roll(col_recv[phase, c, 0], 2, 1))
+        halo = pltpu.roll(halo, 4, 0)
         sea_now = sea[...]
-
-        def one(il, carry):
-            halo, m0, m1 = carry
+        acc = jnp.zeros((8, 128), jnp.float32)
+        m0, m1 = sums
+        chunk = pl.multiple_of(c * RPC, 8)
+        for il in range(IC):
             i = c * IC + il
-            base = pl.multiple_of(i * RPI, 8)
-            at = pl.multiple_of(il * ND, 8)
+            base = chunk + il * RPI
+            at = il * ND
             speed = courant[i] * sea_now
             keep = [sea_now - speed * float(k) for k in (np.abs(COS[:4]) + np.abs(SIN[:4]))]
             total = jnp.zeros((8, 128), jnp.float32)
@@ -235,7 +279,8 @@
             for m in range(HALF):
                 pos = src[pl.ds(base + 8 * FROM_WEST[m], 8), :]
                 neg = src[pl.ds(base + 8 * FROM_EAST[m], 8), :]
-                edge = jnp.broadcast_to(halo[:, m : m + 1], (8, 128))
+                n = il * HALF + m
+                edge = pltpu.roll(halo, 126 - n, 1)
                 rolled_pos = pltpu.roll(pos, 1, 1)
                 rolled_neg = pltpu.roll(neg, 127, 1)
                 swap = pltpu.roll(jnp.where(first_lane, rolled_pos, rolled_neg), 4, 0)
@@ -243,27 +288,39 @@
                 side_neg = jnp.where(last_lane, jnp.where(low, swap, edge), rolled_neg)
                 new_pos = step(FROM_WEST[m], pos, side_pos)
                 new_neg = step(FROM_EAST[m], neg, side_neg)
-                if phase == 1:
+                if phase == 0:
+                    acc = put(acc, n, new_pos, new_neg)
+                else:
                     total = total + (new_pos + new_neg)
             if phase == 1:
                 m0 = m0 + table[0, i] * total
                 m1 = m1 + table[1, i] * total
-            return pltpu.roll(halo, HALF, 1), m0, m1
-
-        _, m0, m1 = lax.fori_loop(0, IC, one, (halo,) + sums, unroll=True)
+        if phase == 0:
+            receive_corners(c)
+            rate = jnp.zeros((8, 128), jnp.float32)
+            for il in range(IC):
+                inside = (spot >= il * HALF) & (spot < (il + 1) * HALF)
+                rate = jnp.where(inside, courant[c * IC + il], rate)
+            corner = jnp.where(
+                south,
+                pltpu.roll(corner_recv[c, 0], 5, 0),
+                pltpu.roll(corner_recv[c, 1], 3, 0),
+            )
+            col_send[1, c] = acc + rate * (turn[...] * corner)
         return m0, m1
 
     zero = jnp.zeros((8, 128), jnp.float32)
 
     def first_step(c, carry):
         advance(e0, e1, 0, c, (zero, zero))
+        send_cols(1, c)
         pack_rows(e1, 1, c)
         send_rows(1, c)
         return carry
 
     lax.fori_loop(0, CH, first_step, 0)
 
-    def first_edge(c, carry):
+    def first_edge(c):
         receive_rows(0, c)
 
         def one(il, carry):
@@ -281,13 +338,9 @@
             return carry
 
         lax.fori_loop(0, IC, one, 0, unroll=True)
-        pack_cols(e1, 1, c)
-        send_cols(1, c)
-        return carry
-
-    lax.fori_loop(0, CH, first_edge, 0)
 
     def second_step(c, sums):
+        first_edge(c)
         sums = advance(e1, e0, 1, c, sums)
         store(c).start()
         return sums
@@ -307,6 +360,15 @@
 
             cols_to(phase, c, 0).wait_send()
             cols_to(phase, c, 1).wait_send()
+
+        @pl.when(has_north)
+        def _():
+            corners_to(c, 0).wait_send()
+
+        @pl.when(has_south)
+        def _():
+            corners_to(c, 1).wait_send()
+
         store(c).wait()
         return carry
 
@@ -411,11 +473,15 @@
             pltpu.VMEM((2, CH, 2, rows, 128), jnp.float32),
             pltpu.VMEM((2, CH, 8, 128), jnp.float32),
             pltpu.VMEM((2, CH, 2, 8, 128), jnp.float32),
+            pltpu.VMEM((CH, 2, 8, 128), jnp.float32),
+            pltpu.VMEM((8, 128), jnp.float32),
             sem((CH,)),
             sem((CH,)),
             sem((2,)),
             sem((2, CH, 4)),
             sem((2, CH, 4)),
+            sem((CH, 2)),
+            sem((CH, 2)),
         ],
         compiler_params=pltpu.CompilerParams(
             collective_id=0, has_side_effects=True, vmem_limit_bytes=60 * 1024 * 1024

time: 21.2 us -> 20 us (0.943)
  the two profiles are of different devices: /device:TPU:0 before, /device:TPU:1 now
where the time goes in v7:
time: 20 us; the launch traced here: 19.7 us
  Pallas kernels  19.7 us (98%)
    pallas_call x1, Pallas kernels, on_device(): pl.pallas_call(functools.partial(kernel, n_strip, n_pt), out_shape=[whole...  16.7 us
    pallas_call x1, Pallas kernels, on_device(): pl.pallas_call(source_kernel, out_shape=whole, in_specs=[hbm] * 5, out_sp...  3.02 us

profile of v7, /device:TPU:1, one launch (start us, length us, event | category | flops | bytes accessed | tf_op | source)
XLA Modules:
  0.0 19.7 jit_solution(12986616151456033811)
XLA Ops:
  0.0 16.7 %shard_map.64 = (f32[4800,128]{1,0:T(8,128)}, f32[8,128]{1,0:T(8,128)}) custom-call(f32[25]{0:T(128)} %courant_in.1, s32[8,128]{1,0:T(8,128)} %bitcast.31, f32[4800,128]{1,0:T(8,128)} %bitcast.30), custom_call_target="tpu_custom_call" | custom-call | flops 18432000 | bytes 4915200 | tf_op jit(solution)/shard_map/pallas_call | solution.py:459
  16.7 3.0 %shard_map.65 = f32[4800,128]{1,0:T(8,128)} custom-call(f32[8,128]{1,0:T(8,128)} %bitcast.32, f32[8,128]{1,0:T(8,128)} %bitcast.33, s32[8,128]{1,0:T(8,128)} %bitcast.34, f32[8,128]{1,0:T(8,128)} %get-tuple-element.7.mean_ratio_in, f32[4800,128]{1,0:T(8,128)} %get-tuple-element.8.energy), custom_call_target="tpu_custom_call" | custom-call | flops 2457600 | bytes 4915200 | tf_op jit(solution)/shard_map/pallas_call | solution.py:493

commit v8 on v3

--- a/solution.py
+++ b/solution.py
@@ -31,10 +31,10 @@
 
 def kernel(
     n_strip, n_pt,
-    courant_in, sea_in, spectra,
-    out, mean_ratio,
-    e0, e1, sea_mask, sea, courant, table, rise,
-    row_send, row_recv, col_send, col_recv,
+    courant_in, sea_in, wind_speed_in, wind_dir_in, ice_in, spectra,
+    out, mean_out, gain_out,
+    e0, e1, sea_mask, sea, courant, table, wind_speed, wind_dir, ice_mask,
+    row_send, row_recv, col_send, col_recv, gain, mean,
     in_sem, out_sem, small_sem, send_sem, recv_sem,
 ):
     s = lax.axis_index("strip")
@@ -101,7 +101,13 @@
     smalls = [
         pltpu.make_async_copy(source, target, small_sem.at[n])
         for n, (source, target) in enumerate(
-            ((courant_in, courant), (sea_in, sea_mask))
+            (
+                (courant_in, courant),
+                (sea_in, sea_mask),
+                (wind_speed_in, wind_speed),
+                (wind_dir_in, wind_dir),
+                (ice_in, ice_mask),
+            )
         )
     ]
     for c in range(CH):
@@ -132,9 +138,6 @@
     for i in range(NF):
         table[0, i] = float(WEIGHT[i])
         table[1, i] = float(WEIGHT[i] * RATIO[i])
-    for d in range(HALF):
-        rise[pl.ds(d, 1), :] = jnp.full((1, 128), float(abs(SIN[d])), jnp.float32)
-        rise[pl.ds(16 + d, 1), :] = jnp.full((1, 128), float(abs(SIN[HALF + d])), jnp.float32)
     lane = lax.broadcasted_iota(jnp.int32, (8, 128), 1)
     sub = lax.broadcasted_iota(jnp.int32, (8, 128), 0)
     low = sub < 4
@@ -154,41 +157,37 @@
 
         lax.fori_loop(0, IC, one, 0, unroll=True)
 
-    def put(acc, m, rolled_pos, neg):
-        mixed = jnp.where(low, neg, rolled_pos)
-        if m:
-            mixed = pltpu.roll(mixed, m, 1)
-        return jnp.where(lane == m, mixed, acc)
+    spot = jnp.where(low, lane - 1, lane)
+
+    def put(acc, n, pos, neg):
+        mixed = pltpu.roll(jnp.where(low, neg, pos), n + 1, 1)
+        return jnp.where(spot == n, mixed, acc)
 
     def pack_cols(src, phase, c):
-        def one(il, acc):
-            base = pl.multiple_of((c * IC + il) * RPI, 8)
-            own = jnp.zeros((8, 128), jnp.float32)
+        base = pl.multiple_of(c * RPC, 8)
+        acc = jnp.zeros((8, 128), jnp.float32)
+        for il in range(IC):
             for m in range(HALF):
-                pos = src[pl.ds(base + 8 * FROM_WEST[m], 8), :]
-                neg = src[pl.ds(base + 8 * FROM_EAST[m], 8), :]
-                own = put(own, m, pltpu.roll(pos, 1, 1), neg)
-            return jnp.where(lane < HALF, own, pltpu.roll(acc, HALF, 1))
-
-        col_send[phase, c] = lax.fori_loop(
-            0, IC, one, jnp.zeros((8, 128), jnp.float32), unroll=True
-        )
+                pos = src[pl.ds(base + il * RPI + 8 * FROM_WEST[m], 8), :]
+                neg = src[pl.ds(base + il * RPI + 8 * FROM_EAST[m], 8), :]
+                acc = put(acc, il * HALF + m, pos, neg)
+        col_send[phase, c] = acc
 
     load(0).wait()
-    pack_cols(e0, 0, 0)
     pack_rows(e0, 0, 0)
     pl.semaphore_wait(
         barrier, 2 + has_north.astype(jnp.int32) + has_south.astype(jnp.int32)
     )
+    send_rows(0, 0)
+    pack_cols(e0, 0, 0)
     send_cols(0, 0)
-    send_rows(0, 0)
 
     def first_halo(c, carry):
         load(c).wait()
+        pack_rows(e0, 0, c)
+        send_rows(0, c)
         pack_cols(e0, 0, c)
         send_cols(0, c)
-        pack_rows(e0, 0, c)
-        send_rows(0, c)
         return carry
 
     lax.fori_loop(1, CH, first_halo, 0)
@@ -196,19 +195,29 @@
         small.wait()
     sea[...] = sea_mask[...].astype(jnp.float32)
 
+    strength = (1.0 - ice_mask[...].astype(jnp.float32)) * 0.05 * wind_speed[...]
+    cos_wind = strength * jnp.cos(wind_dir[...])
+    sin_wind = strength * jnp.sin(wind_dir[...])
+    for d in range(ND):
+        gain[pl.ds(8 * d, 8), :] = jnp.maximum(
+            float(COS[d]) * cos_wind + float(SIN[d]) * sin_wind, 0.0
+        )
+    gain_copy = pltpu.make_async_copy(gain, gain_out, small_sem.at[0])
+    gain_copy.start()
+
     def advance(src, dst, phase, c, sums):
         receive_cols(phase, c)
-        if phase == 1:
-            receive_rows(phase, c)
-        halo = pltpu.roll(jnp.where(low, col_recv[phase, c, 1], col_recv[phase, c, 0]), 4, 0)
-        halo = pltpu.roll(halo, 128 - (IC - 1) * HALF, 1)
+        receive_rows(phase, c)
+        halo = jnp.where(low, col_recv[phase, c, 1], pltpu.roll(col_recv[phase, c, 0], 2, 1))
+        halo = pltpu.roll(halo, 4, 0)
         sea_now = sea[...]
-
-        def one(il, carry):
-            halo, m0, m1 = carry
+        acc = jnp.zeros((8, 128), jnp.float32)
+        m0, m1 = sums
+        chunk = pl.multiple_of(c * RPC, 8)
+        for il in range(IC):
             i = c * IC + il
-            base = pl.multiple_of(i * RPI, 8)
-            at = pl.multiple_of(il * ND, 8)
+            base = chunk + il * RPI
+            at = il * ND
             speed = courant[i] * sea_now
             keep = [sea_now - speed * float(k) for k in (np.abs(COS[:4]) + np.abs(SIN[:4]))]
             total = jnp.zeros((8, 128), jnp.float32)
@@ -220,12 +229,9 @@
                 else:
                     near = pltpu.roll(core, 7, 0)
                     r0, r1, way, m = 3, 7, 1, d - HALF
-                if phase == 0:
-                    near = jnp.where((sub == r0) | (sub == r1), 0.0, near)
-                else:
-                    h0 = row_recv[phase, c, way, pl.ds(at + m, 1), :]
-                    h1 = row_recv[phase, c, way, pl.ds(at + HALF + m, 1), :]
-                    near = jnp.where(sub == r0, h0, jnp.where(sub == r1, h1, near))
+                h0 = row_recv[phase, c, way, pl.ds(at + m, 1), :]
+                h1 = row_recv[phase, c, way, pl.ds(at + HALF + m, 1), :]
+                near = jnp.where(sub == r0, h0, jnp.where(sub == r1, h1, near))
                 flow = float(abs(COS[d])) * side + float(abs(SIN[d])) * near
                 q = d % 6
                 fresh = keep[q if q < 4 else 6 - q] * core + speed * flow
@@ -235,7 +241,8 @@
             for m in range(HALF):
                 pos = src[pl.ds(base + 8 * FROM_WEST[m], 8), :]
                 neg = src[pl.ds(base + 8 * FROM_EAST[m], 8), :]
-                edge = jnp.broadcast_to(halo[:, m : m + 1], (8, 128))
+                n = il * HALF + m
+                edge = pltpu.roll(halo, 126 - n, 1)
                 rolled_pos = pltpu.roll(pos, 1, 1)
                 rolled_neg = pltpu.roll(neg, 127, 1)
                 swap = pltpu.roll(jnp.where(first_lane, rolled_pos, rolled_neg), 4, 0)
@@ -243,49 +250,27 @@
                 side_neg = jnp.where(last_lane, jnp.where(low, swap, edge), rolled_neg)
                 new_pos = step(FROM_WEST[m], pos, side_pos)
                 new_neg = step(FROM_EAST[m], neg, side_neg)
-                if phase == 1:
+                if phase == 0:
+                    acc = put(acc, n, new_pos, new_neg)
+                else:
                     total = total + (new_pos + new_neg)
             if phase == 1:
                 m0 = m0 + table[0, i] * total
                 m1 = m1 + table[1, i] * total
-            return pltpu.roll(halo, HALF, 1), m0, m1
-
-        _, m0, m1 = lax.fori_loop(0, IC, one, (halo,) + sums, unroll=True)
+        if phase == 0:
+            col_send[1, c] = acc
         return m0, m1
 
     zero = jnp.zeros((8, 128), jnp.float32)
 
     def first_step(c, carry):
         advance(e0, e1, 0, c, (zero, zero))
+        send_cols(1, c)
         pack_rows(e1, 1, c)
         send_rows(1, c)
         return carry
 
     lax.fori_loop(0, CH, first_step, 0)
-
-    def first_edge(c, carry):
-        receive_rows(0, c)
-
-        def one(il, carry):
-            i = c * IC + il
-            base = pl.multiple_of(i * RPI, 8)
-            at = pl.multiple_of(il * ND, 8)
-            for way in range(2):
-                for tile, first, count, to in pieces():
-                    row = 4 * tile + 3 * way
-                    rows = pl.ds(base + (HALF * way + first) * 8 + row, count, stride=8)
-                    speed = courant[i] * sea[pl.ds(row, 1), :]
-                    term = row_recv[0, c, way, pl.ds(at + to, count), :]
-                    term = term * rise[pl.ds(16 * way + first, count), :]
-                    e1[rows, :] = e1[rows, :] + speed * term
-            return carry
-
-        lax.fori_loop(0, IC, one, 0, unroll=True)
-        pack_cols(e1, 1, c)
-        send_cols(1, c)
-        return carry
-
-    lax.fori_loop(0, CH, first_edge, 0)
 
     def second_step(c, sums):
         sums = advance(e1, e0, 1, c, sums)
@@ -293,7 +278,9 @@
         return sums
 
     m0, m1 = lax.fori_loop(0, CH, second_step, (zero, zero))
-    mean_ratio[...] = m1 / jnp.maximum(m0, 0.05)
+    mean[...] = m1 / jnp.maximum(m0, 0.05)
+    mean_copy = pltpu.make_async_copy(mean, mean_out, small_sem.at[1])
+    mean_copy.start()
 
     def finish(c, carry):
         for phase in range(2):
@@ -307,16 +294,19 @@
 
             cols_to(phase, c, 0).wait_send()
             cols_to(phase, c, 1).wait_send()
+
         store(c).wait()
         return carry
 
     lax.fori_loop(0, CH, finish, 0)
+    gain_copy.wait()
+    mean_copy.wait()
 
 
 def source_kernel(
-    wind_speed_in, wind_dir_in, ice_in, mean_ratio_in, energy,
+    gain_in, ice_in, mean_ratio_in, energy,
     out,
-    held, done, wind_speed, wind_dir, ice_mask, mean_ratio, gain,
+    held, done, gain, ice_mask, mean_ratio,
     in_sem, out_sem, small_sem,
 ):
     loads = [
@@ -335,10 +325,9 @@
         pltpu.make_async_copy(source, target, small_sem.at[n])
         for n, (source, target) in enumerate(
             (
-                (wind_dir_in, wind_dir),
-                (wind_speed_in, wind_speed),
+                (mean_ratio_in, mean_ratio),
                 (ice_in, ice_mask),
-                (mean_ratio_in, mean_ratio),
+                (gain_in, gain),
             )
         )
     ]
@@ -347,13 +336,6 @@
     for copy in smalls:
         copy.wait()
     ice = ice_mask[...].astype(jnp.float32)
-    strength = (1.0 - ice) * 0.05 * wind_speed[...]
-    cos_wind = strength * jnp.cos(wind_dir[...])
-    sin_wind = strength * jnp.sin(wind_dir[...])
-    for d in range(ND):
-        gain[pl.ds(8 * d, 8), :] = jnp.maximum(
-            float(COS[d]) * cos_wind + float(SIN[d]) * sin_wind, 0.0
-        )
     drag = 0.02 * mean_ratio[...]
     cold = 0.7 * ice
     for c in range(CH):
@@ -388,17 +370,16 @@
 
 def on_device(n_strip, n_pt, spectra, courant, wind_speed, wind_dir, sea_mask, ice_mask):
     total = spectra.shape[0] * 8
-    vmem = pl.BlockSpec(memory_space=pltpu.VMEM)
     hbm = pl.BlockSpec(memory_space=pl.ANY)
     sem = pltpu.SemaphoreType.DMA
     rows = IC * ND
     whole = jax.ShapeDtypeStruct((total, 128), jnp.float32)
     point = jax.ShapeDtypeStruct((8, 128), jnp.float32)
-    energy, mean_ratio = pl.pallas_call(
+    energy, mean_ratio, gain = pl.pallas_call(
         functools.partial(kernel, n_strip, n_pt),
-        out_shape=[whole, point],
-        in_specs=[hbm] * 3,
-        out_specs=[hbm, vmem],
+        out_shape=[whole, point, jax.ShapeDtypeStruct((ND * 8, 128), jnp.float32)],
+        in_specs=[hbm] * 6,
+        out_specs=[hbm] * 3,
         scratch_shapes=[
             pltpu.VMEM((total, 128), jnp.float32),
             pltpu.VMEM((total, 128), jnp.float32),
@@ -406,14 +387,18 @@
             pltpu.VMEM((8, 128), jnp.float32),
             pltpu.SMEM((NF,), jnp.float32),
             pltpu.SMEM((2, NF), jnp.float32),
-            pltpu.VMEM((32, 128), jnp.float32),
+            pltpu.VMEM((8, 128), jnp.float32),
+            pltpu.VMEM((8, 128), jnp.float32),
+            pltpu.VMEM((8, 128), jnp.int32),
             pltpu.VMEM((2, CH, 2, rows, 128), jnp.float32),
             pltpu.VMEM((2, CH, 2, rows, 128), jnp.float32),
             pltpu.VMEM((2, CH, 8, 128), jnp.float32),
             pltpu.VMEM((2, CH, 2, 8, 128), jnp.float32),
+            pltpu.VMEM((ND * 8, 128), jnp.float32),
+            pltpu.VMEM((8, 128), jnp.float32),
             sem((CH,)),
             sem((CH,)),
-            sem((2,)),
+            sem((5,)),
             sem((2, CH, 4)),
             sem((2, CH, 4)),
         ],
@@ -423,31 +408,35 @@
         cost_estimate=pl.CostEstimate(
             flops=30 * total * 128, bytes_accessed=8 * total * 128, transcendentals=0
         ),
-    )(courant, to_tiles(sea_mask[None]), to_tiles(spectra))
+    )(
+        courant,
+        to_tiles(sea_mask[None]),
+        to_tiles(wind_speed[None]),
+        to_tiles(wind_dir[None]),
+        to_tiles(ice_mask[None]),
+        to_tiles(spectra),
+    )
     result = pl.pallas_call(
         source_kernel,
         out_shape=whole,
-        in_specs=[hbm] * 5,
+        in_specs=[hbm] * 4,
         out_specs=hbm,
         scratch_shapes=[
             pltpu.VMEM((total, 128), jnp.float32),
             pltpu.VMEM((total, 128), jnp.float32),
-            pltpu.VMEM((8, 128), jnp.float32),
-            pltpu.VMEM((8, 128), jnp.float32),
+            pltpu.VMEM((ND * 8, 128), jnp.float32),
             pltpu.VMEM((8, 128), jnp.int32),
             pltpu.VMEM((8, 128), jnp.float32),
-            pltpu.VMEM((ND * 8, 128), jnp.float32),
             sem((CH,)),
             sem((CH,)),
-            sem((4,)),
+            sem((3,)),
         ],
         compiler_params=pltpu.CompilerParams(vmem_limit_bytes=60 * 1024 * 1024),
         cost_estimate=pl.CostEstimate(
             flops=4 * total * 128, bytes_accessed=8 * total * 128, transcendentals=total * 128
         ),
     )(
-        to_tiles(wind_speed[None]),
-        to_tiles(wind_dir[None]),
+        gain,
         to_tiles(ice_mask[None]),
         mean_ratio,
         energy,

time: 21.2 us -> 18.3 us (0.86)
  the two profiles are of different devices: /device:TPU:0 before, /device:TPU:1 now
where the time goes in v8:
time: 18.3 us; the launch traced here: 18.1 us
  Pallas kernels  18.1 us (99%)
    pallas_call x1, Pallas kernels, on_device(): pl.pallas_call(functools.partial(kernel, n_strip, n_pt), out_shape=[whole...  15 us
    pallas_call x1, Pallas kernels, on_device(): pl.pallas_call(source_kernel, out_shape=whole, in_specs=[hbm] * 4, out_sp...  3.15 us

profile of v8, /device:TPU:1, one launch (start us, length us, event | category | flops | bytes accessed | tf_op | source)
XLA Modules:
  0.0 18.1 jit_solution(11046053116293904460)
XLA Ops:
  0.0 15.0 %shard_map.64 = (f32[4800,128]{1,0:T(8,128)}, f32[8,128]{1,0:T(8,128)}, f32[192,128]{1,0:T(8,128)}) custom-call(f32[25]{0:T(128)} %courant_in.1, s32[8,128]{1,0:T(8,128)} %bitcast.33, f32[8,128]{1,0:T(8,128)} %bitcast.34, f32[8,128]{1,0:T(8,128)} %bitcast.35, s32[8,128]{1,0:T(8,128)} %bitcast.31, f32[4800,128]{1,0:T(8,128)} %bitcast.30), custom_call_target="tpu_custom_call" | custom-call | flops 18432000 | bytes 4915200 | tf_op jit(solution)/shard_map/pallas_call | solution.py:378
  15.0 3.1 %shard_map.65 = f32[4800,128]{1,0:T(8,128)} custom-call(f32[192,128]{1,0:T(8,128)} %get-tuple-element.8.gain_in, s32[8,128]{1,0:T(8,128)} %bitcast.32, f32[8,128]{1,0:T(8,128)} %get-tuple-element.9.mean_ratio_in, f32[4800,128]{1,0:T(8,128)} %get-tuple-element.10.energy), custom_call_target="tpu_custom_call" | custom-call | flops 2457600 | bytes 4915200 | tf_op jit(solution)/shard_map/pallas_call | solution.py:419

commit v9 on v8

--- a/solution.py
+++ b/solution.py
@@ -306,21 +306,17 @@
 def source_kernel(
     gain_in, ice_in, mean_ratio_in, energy,
     out,
-    held, done, gain, ice_mask, mean_ratio,
+    held, done, gain, ice_mask, mean_ratio, table,
     in_sem, out_sem, small_sem,
 ):
-    loads = [
-        pltpu.make_async_copy(
-            energy.at[pl.ds(c * RPC, RPC), :], held.at[pl.ds(c * RPC, RPC), :], in_sem.at[c]
-        )
-        for c in range(CH)
-    ]
-    stores = [
-        pltpu.make_async_copy(
-            done.at[pl.ds(c * RPC, RPC), :], out.at[pl.ds(c * RPC, RPC), :], out_sem.at[c]
-        )
-        for c in range(CH)
-    ]
+    def load(c):
+        rows = pl.ds(c * RPC, RPC)
+        return pltpu.make_async_copy(energy.at[rows, :], held.at[rows, :], in_sem.at[c])
+
+    def store(c):
+        rows = pl.ds(c * RPC, RPC)
+        return pltpu.make_async_copy(done.at[rows, :], out.at[rows, :], out_sem.at[c])
+
     smalls = [
         pltpu.make_async_copy(source, target, small_sem.at[n])
         for n, (source, target) in enumerate(
@@ -331,29 +327,35 @@
             )
         )
     ]
-    for copy in smalls + loads:
+    load(0).start()
+    for copy in smalls:
         copy.start()
+    for c in range(1, CH):
+        load(c).start()
+    for i in range(NF):
+        table[i] = float(RATIO[i])
     for copy in smalls:
         copy.wait()
     ice = ice_mask[...].astype(jnp.float32)
     drag = 0.02 * mean_ratio[...]
     cold = 0.7 * ice
+
+    def chunk(c, carry):
+        load(c).wait()
+        base = pl.multiple_of(c * RPC, 8)
+        ratios = [table[c * IC + il] for il in range(IC)]
+        losses = [ratio * drag + cold for ratio in ratios]
+        for d in range(ND):
+            push = gain[pl.ds(8 * d, 8), :]
+            for il in range(IC):
+                rows = pl.ds(base + il * RPI + 8 * d, 8)
+                done[rows, :] = held[rows, :] * jnp.exp(ratios[il] * push - losses[il])
+        store(c).start()
+        return carry
+
+    lax.fori_loop(0, CH, chunk, 0)
     for c in range(CH):
-        loads[c].wait()
-        losses = [float(RATIO[c * IC + il]) * drag + cold for il in range(IC)]
-
-        def one(d, carry):
-            push = gain[pl.ds(pl.multiple_of(8 * d, 8), 8), :]
-            for il in range(IC):
-                rows = pl.ds(pl.multiple_of((c * IC + il) * RPI + 8 * d, 8), 8)
-                net = float(RATIO[c * IC + il]) * push - losses[il]
-                done[rows, :] = held[rows, :] * jnp.exp(net)
-            return carry
-
-        lax.fori_loop(0, ND, one, 0, unroll=8)
-        stores[c].start()
-    for copy in stores:
-        copy.wait()
+        store(c).wait()
 
 
 def to_tiles(x):
@@ -427,6 +429,7 @@
             pltpu.VMEM((ND * 8, 128), jnp.float32),
             pltpu.VMEM((8, 128), jnp.int32),
             pltpu.VMEM((8, 128), jnp.float32),
+            pltpu.SMEM((NF,), jnp.float32),
             sem((CH,)),
             sem((CH,)),
             sem((3,)),

time: 18.3 us -> 18.3 us (level)
  no operation moved by 1% of the time
where the time goes in v9:
time: 18.3 us; the launch traced here: 18.1 us
  Pallas kernels  18.1 us (99%)
    pallas_call x1, Pallas kernels, on_device(): pl.pallas_call(functools.partial(kernel, n_strip, n_pt), out_shape=[whole...  15 us
    pallas_call x1, Pallas kernels, on_device(): pl.pallas_call(source_kernel, out_shape=whole, in_specs=[hbm] * 4, out_sp...  3.13 us

profile of v9, /device:TPU:1, one launch (start us, length us, event | category | flops | bytes accessed | tf_op | source)
XLA Modules:
  0.0 18.1 jit_solution(14228192741771665901)
XLA Ops:
  0.0 15.0 %shard_map.64 = (f32[4800,128]{1,0:T(8,128)}, f32[8,128]{1,0:T(8,128)}, f32[192,128]{1,0:T(8,128)}) custom-call(f32[25]{0:T(128)} %courant_in.1, s32[8,128]{1,0:T(8,128)} %bitcast.33, f32[8,128]{1,0:T(8,128)} %bitcast.34, f32[8,128]{1,0:T(8,128)} %bitcast.35, s32[8,128]{1,0:T(8,128)} %bitcast.31, f32[4800,128]{1,0:T(8,128)} %bitcast.30), custom_call_target="tpu_custom_call" | custom-call | flops 18432000 | bytes 4915200 | tf_op jit(solution)/shard_map/pallas_call | solution.py:380
  15.0 3.1 %shard_map.65 = f32[4800,128]{1,0:T(8,128)} custom-call(f32[192,128]{1,0:T(8,128)} %get-tuple-element.8.gain_in, s32[8,128]{1,0:T(8,128)} %bitcast.32, f32[8,128]{1,0:T(8,128)} %get-tuple-element.9.mean_ratio_in, f32[4800,128]{1,0:T(8,128)} %get-tuple-element.10.energy), custom_call_target="tpu_custom_call" | custom-call | flops 2457600 | bytes 4915200 | tf_op jit(solution)/shard_map/pallas_call | solution.py:421

commit v10 on v8

--- a/solution.py
+++ b/solution.py
@@ -73,11 +73,15 @@
         )
 
     def send_rows(phase, c):
+        @pl.when(has_south & (lax.rem(s, 2) == 0))
+        def _():
+            rows_to(phase, c, 1).start()
+
         @pl.when(has_north)
         def _():
             rows_to(phase, c, 0).start()
 
-        @pl.when(has_south)
+        @pl.when(has_south & (lax.rem(s, 2) == 1))
         def _():
             rows_to(phase, c, 1).start()
 

time: 18.3 us -> 18.3 us (level)
  no operation moved by 1% of the time
where the time goes in v10:
time: 18.3 us; the launch traced here: 18.1 us
  Pallas kernels  18.1 us (99%)
    pallas_call x1, Pallas kernels, on_device(): pl.pallas_call(functools.partial(kernel, n_strip, n_pt), out_shape=[whole...  15 us
    pallas_call x1, Pallas kernels, on_device(): pl.pallas_call(source_kernel, out_shape=whole, in_specs=[hbm] * 4, out_sp...  3.15 us

profile of v10, /device:TPU:1, one launch (start us, length us, event | category | flops | bytes accessed | tf_op | source)
XLA Modules:
  0.0 18.1 jit_solution(18086069092011298038)
XLA Ops:
  0.0 15.0 %shard_map.64 = (f32[4800,128]{1,0:T(8,128)}, f32[8,128]{1,0:T(8,128)}, f32[192,128]{1,0:T(8,128)}) custom-call(f32[25]{0:T(128)} %courant_in.1, s32[8,128]{1,0:T(8,128)} %bitcast.33, f32[8,128]{1,0:T(8,128)} %bitcast.34, f32[8,128]{1,0:T(8,128)} %bitcast.35, s32[8,128]{1,0:T(8,128)} %bitcast.31, f32[4800,128]{1,0:T(8,128)} %bitcast.30), custom_call_target="tpu_custom_call" | custom-call | flops 18432000 | bytes 4915200 | tf_op jit(solution)/shard_map/pallas_call | solution.py:382
  15.0 3.1 %shard_map.65 = f32[4800,128]{1,0:T(8,128)} custom-call(f32[192,128]{1,0:T(8,128)} %get-tuple-element.8.gain_in, s32[8,128]{1,0:T(8,128)} %bitcast.32, f32[8,128]{1,0:T(8,128)} %get-tuple-element.9.mean_ratio_in, f32[4800,128]{1,0:T(8,128)} %get-tuple-element.10.energy), custom_call_target="tpu_custom_call" | custom-call | flops 2457600 | bytes 4915200 | tf_op jit(solution)/shard_map/pallas_call | solution.py:423
